TPU v7x, 128 devices: a whole 4x4x4 slice. The times are simulated.
128 devices in a mesh: users: 16 (over z, x), items: 8 (over y, core).
Axes of the slice: x: 4, y: 4, z: 4, core: 2. Of those that a mesh axis runs over, the one named last changes fastest.
Arguments:
- interactions: bfloat16 [32768, 32768], P('users', 'items'), may hold values from 0 to 13, as said below
- user_weights: bfloat16 [32768], P('users'), may hold values from 0.3 to 9, as said below
- panel_index: int32 [1], replicated, may hold values from 0 to 127
Outputs:
- item_covariance: float32 [8, 4096, 256], P(None, ('users', 'items'))
- item_mean: float32 [8, 4096], P(None, ('users', 'items'))
Inputs may be any that keep to these rules, and one draw needn't show every extreme that they name: `user_weights`: positive user weights. `interactions`: confidences are zero or positive.
All inputs are finite; a program needn't handle non-finite values.
Results may differ from a plain program's by a relative error of at most 0.00031.
Values may be sent and summed in bfloat16 or wider, within the bound.
No kernel may reach another device: no remote copies, remote signals or barrier semaphores. Data moves between devices by JAX's collectives and lax.ppermute only.
A program may use at most 384 MiB of HBM per device.

v0:
```python
import jax
import jax.numpy as jnp
from jax import lax
from jax.sharding import PartitionSpec as P

P_SIZE = 256
BLK = 32


def from_root(block, axis, source):
    block = jnp.where(lax.axis_index(axis) == source, block, jnp.zeros_like(block))
    return lax.psum(block, axis)


def combined_all(value, axis, join):
    pieces = jax.tree.map(lambda part: lax.all_gather(part, axis), value)
    head = jax.tree.map(lambda part: part[0], pieces)
    tail = jax.tree.map(lambda part: part[1:], pieces)
    total, _ = lax.scan(lambda total, slab: (join(total, slab), None), head, tail)
    return total


def chan_combine(left, right):
    count_a, mean_a, panel_a, moment_a = left
    count_b, mean_b, panel_b, moment_b = right
    total = count_a + count_b
    factor = count_b / total
    delta = mean_b - mean_a
    panel_delta = panel_b - panel_a
    moment = moment_a + moment_b + count_a * count_b / total * delta[:, None] * panel_delta[None, :]
    return (total, mean_a + factor * delta, panel_a + factor * panel_delta, moment)


def contract_users(left, right):
    return lax.dot_general(
        left, right, (((0,), (0,)), ((), ())), preferred_element_type=jnp.float32
    )


def per_device(interactions, user_weights, panel_index):
    shard_rows = interactions.shape[1]
    per_shard = shard_rows // P_SIZE
    chosen = panel_index[0]
    owner = chosen // per_shard
    local_cols = lax.dynamic_slice_in_dim(interactions, chosen % per_shard * P_SIZE, P_SIZE, 1)
    panel = from_root(local_cols, "items", owner)
    weights32 = user_weights.astype(jnp.float32)
    weighted = (weights32[:, None] * panel.astype(jnp.float32)).astype(jnp.bfloat16)
    gram = contract_users(interactions, weighted)
    colsum = contract_users(interactions, user_weights)
    panel_sum = contract_users(user_weights, panel)
    count = jnp.sum(weights32).reshape(1)
    users_count = lax.axis_size("users")
    items_count = lax.axis_size("items")
    cycles_local = shard_rows // (users_count * items_count * BLK)
    tile_shape = (cycles_local, users_count, items_count, BLK, P_SIZE)
    mean_local = colsum / count
    panel_local = panel_sum / count
    moment = gram - mean_local[:, None] * panel_sum[None, :]
    total, mean_all, panel_all, moment_all = combined_all(
        (count, mean_local, panel_local, moment), "users", chan_combine
    )
    rank = lax.axis_index("users")
    own_moment = lax.dynamic_slice_in_dim(moment_all.reshape(tile_shape), rank, 1, 1)
    covar = own_moment / total
    mean_part = lax.dynamic_slice_in_dim(mean_all.reshape(tile_shape[:4]), rank, 1, 1)
    moved_cov, moved_mean = (
        lax.all_to_all(covar, "items", split_axis=2, concat_axis=0, tiled=True),
        lax.all_to_all(mean_part, "items", split_axis=2, concat_axis=0, tiled=True),
    )
    return (moved_cov.reshape(-1, BLK, P_SIZE), moved_mean.reshape(-1, BLK))


def solution(mesh):
    return jax.shard_map(
        per_device,
        mesh=mesh,
        in_specs=(P("users", "items"), P("users"), P()),
        out_specs=(P(None, ("users", "items"), None), P(None, ("users", "items"))),
        check_vma=False,
    )
```

profile of v0, /device:TPU:1, one launch (start us, length us, event | category | flops | bytes accessed | tf_op | source)
XLA Modules:
  0.0 744.8 jit_solution(11204003330880511260)
XLA Ops:
  7.9 2.4 dynamic-slice_select_fusion
  11.1 8.0 %fusion.3 = f32[1,4096]{1,0:T(1,128)S(1)} fusion(bf16[2048,4096]{1,0:T(8,128)(2,1)} %param.5, bf16[2048,1]{0,1:T(2,128)(2,1)S(1)} %reshape.68), kind=kOutput, calls=%fused_computation.20 | convolution fusion | flops 16777216 | bytes 16797696 | tf_op jit(solution)/shard_map/dot_general | solution.py:35
  20.3 53.9 %all-reduce.3.cloned.1.call-done = bf16[2048,256]{1,0:T(8,128)(2,1)} async-done(((bf16[2048,256]{1,0:T(8,128)(2,1)}), bf16[2048,256]{1,0:T(8,128)(2,1)}) %all-reduce.3.cloned.1.call-update) | async-done | bytes 1048592 | tf_op jit(solution)/shard_map/psum | solution.py:12
  75.6 12.8 %fusion.1 = f32[4096,256]{0,1:T(8,128)} fusion(bf16[2048,4096]{1,0:T(8,128)(2,1)} %param.5, f32[256]{0:T(256)S(1)} %bitcast.64, f32[4096]{0:T(1024)S(1)} %broadcast_divide_fusion, bf16[2048,256]{1,0:T(8,128)(2,1)} %all-reduce.3.cloned.1.call-done, f32[2048]{0:T(1024)S(1)} %convert_element_type.9), kind=kOutput, calls=%fused_computation.9 | convolution fusion | flops 4298637312 | bytes 22045696 | tf_op jit(solution)/shard_map/dot_general | solution.py:35
  91.0 34.3 %all-reduce = f32[16]{0:T(128)} all-reduce(f32[16]{0:T(128)S(1)} %dynamic-update-slice), channel_id=1, replica_groups=mesh['users'=16,'items'=8] {'users'}, use_global_device_ids=true, to_apply=%add | all-reduce | flops 16 | bytes 128
  125.3 18.2 %all-gather = f32[65536]{0:T(1024)S(1)} all-gather(f32[4096]{0:T(1024)S(1)} %broadcast_divide_fusion), channel_id=2, replica_groups=mesh['users'=16,'items'=8] {'users'}, dimensions={0}, use_global_device_ids=true | all-gather | bytes 278528 | tf_op jit(solution)/shard_map/all_gather | solution.py:16
  144.9 20.1 %all-gather.3 = f32[16,1,256]{2,1,0:T(1,128)S(1)} all-gather(f32[1,1,256]{2,1,0:T(1,128)S(1)} %bitcast.66), channel_id=3, replica_groups=mesh['users'=16,'items'=8] {'users'}, dimensions={0}, use_global_device_ids=true | all-gather | bytes 17408 | tf_op jit(solution)/shard_map/all_gather | solution.py:16
  165.0 295.1 %all-gather.6.cloned.1.call-done = f32[65536,256]{0,1:T(8,128)} async-done(((f32[4096,256]{0,1:T(8,128)}), f32[65536,256]{0,1:T(8,128)}) %all-gather.6.cloned.1.call-update) | async-done | bytes 67108880 | tf_op jit(solution)/shard_map/all_gather | solution.py:16
  460.1 40.8 %slice.47 = f32[61440,256]{0,1:T(8,128)} slice(f32[65536,256]{0,1:T(8,128)} %all-gather.6.cloned.1.call-done), slice={[4096:65536], [0:256]} | slice | bytes 125829120 | tf_op jit(solution)/shard_map/slice | solution.py:18
  500.9 60.9 %copy.11 = f32[61440,256]{1,0:T(8,128)} copy(f32[61440,256]{0,1:T(8,128)} %slice.47) | data formatting | bytes 125829120 | tf_op jit(solution)/shard_map/slice | solution.py:18
  561.8 4.6 slice.44
  566.4 5.6 copy.12
  572.0 143.9 %while.16 = (s32[]{:T(128)}, f32[1]{0:T(128)}, f32[4096]{0:T(1024)S(1)}, f32[256]{0:T(256)S(1)}, f32[4096,256]{1,0:T(8,128)}, /*index=5*/f32[15,1]{0,1:T(1,128)S...) while((s32[]{:T(128)}, f32[1]{0:T(128)}, f32[4096]{0:T(1024)S(1)}, ...), condition=%wide.region_3.4_spmd, body=%wide.region_2.3_spmd.sunk | while | flops 3162886 | bytes 12704961 | solution.py:19
  576.0 5.1 fusion.11
  585.6 5.1 fusion.11
  595.1 5.1 fusion.11
  604.7 5.1 fusion.11
  614.3 5.1 fusion.11
  623.9 5.1 fusion.11
  633.5 5.1 fusion.11
  643.1 5.1 fusion.11
  652.7 5.1 fusion.11
  662.3 5.1 fusion.11
  671.9 5.1 fusion.11
  681.5 5.1 fusion.11
  691.1 5.1 fusion.11
  700.7 5.1 fusion.11
  710.3 5.1 fusion.11
  716.6 5.0 all-to-all-start.1
  721.6 2.3 divide_bitcast_fusion
  726.1 4.0 all-to-all-start
  730.1 6.5 all-to-all-done
  (110 shorter events, 20.9 us)
Async XLA Ops:
  7.2 67.0 %all-reduce.3.cloned.1.call-start = ((), (), s32[]{:S(2)}) async-start(), calls=%async_computation.2 | async-start | bytes 2097152 | tf_op jit(solution)/shard_map/psum | solution.py:12
  10.3 449.8 %all-gather.6.cloned.1.call-start = ((), (), s32[]{:S(2)}) async-start(), calls=%async_computation.3 | async-start | bytes 71303168 | tf_op jit(solution)/shard_map/all_gather | solution.py:16
  11.1 8.1 %copy-start.2 = (bf16[2048]{0:T(1024)(128)(2,1)S(1)}, bf16[2048]{0:T(1024)(128)(2,1)}, u32[]{:S(2)}) copy-start(bf16[2048]{0:T(1024)(128)(2,1)} %param.6) | copy-start | bytes 12292
  88.4 0.7 copy-start.3
  143.5 357.4 %copy-start = (f32[65536]{0:T(1024)}, f32[65536]{0:T(1024)S(1)}, u32[]{:S(2)}) copy-start(f32[65536]{0:T(1024)S(1)} %all-gather) | copy-start | bytes 786436
  165.0 335.9 %copy-start.1 = (f32[16,1,256]{2,1,0:T(1,128)}, f32[16,1,256]{2,1,0:T(1,128)S(1)}, u32[]{:S(2)}) copy-start(f32[16,1,256]{2,1,0:T(1,128)S(1)} %all-gather.3) | copy-start | bytes 49156
  566.4 5.6 slice-start
  566.4 5.6 slice-start.1
  716.6 9.5 %all-to-all-start.1 = ((f32[1,1,8,32]{3,1,0,2:T(1,128)}), f32[1,1,8,32]{3,1,0,2:T(1,128)S(1)}, u32[]{:S(2)}, u32[]{:S(2)}) async-start(f32[1,1,8,32]{3,1,0,2:T(1,128)} %bitcast.20), calls=%async_computation.1 | async-start | bytes 8192 | tf_op jit(solution)/shard_map/all_to_all | solution.py:69
  726.1 10.5 %all-to-all-start = ((f32[1,1,8,32,256]{4,3,1,0,2:T(8,128)}), f32[1,1,8,32,256]{4,3,1,0,2:T(8,128)S(1)}, u32[]{:S(2)}, u32[]{:S(2)}) async-start(f32[1,1,8,32,256]{4,3,1,0,2:T(8,128)} %divide_bitcast_fusion), calls=%async_computation | async-start | bytes 524288 | tf_op jit(solution)/shard_map/all_to_all | solution.py:68
Sparse Core Ops, SparseCore 0:
  10.5 63.6 all-reduce.2
  88.6 371.5 all-gather.5
where the time goes:
time: 747 us; the launch traced here: 745 us
  waiting for transfers between devices  358 us (48%)
  local copies, waits for them, and re-layouts  127 us (17%)
  other arithmetic  83.8 us (11%)
  blocking collectives  72.7 us (10%)
  loops' own time  57.3 us (8%)
  matrix products  22.3 us (3%)
  between operations  14.8 us (2%)
  starting transfers between devices  9.05 us (1%)
    all_gather x1, waiting for transfers between devices, combined_all(): pieces = jax.tree.map(lambda part: lax.all_gather(part, axis), value)  295 us
    slice x6, local copies, waits for them, and re-layouts, combined_all(): tail = jax.tree.map(lambda part: part[1:], pieces)  102 us
    add x15, other arithmetic, chan_combine(): moment_a + moment_b  77.1 us
    another operation x1, loops' own time, combined_all(): lax.scan(lambda total, slab: (join(total, slab), None), head, tail)  57.3 us
    psum x1, waiting for transfers between devices, from_root(): return lax.psum(block, axis)  53.9 us
    all_gather x2, blocking collectives, combined_all(): pieces = jax.tree.map(lambda part: lax.all_gather(part, axis), value)  38.3 us
    unnamed x1, blocking collectives  34.3 us
    dot_general x3, matrix products, contract_users(): lax.dot_general(left, right, (((0,), (0,)), ((), ())), preferred_element_...  22.3 us
  transfers between devices with their start and end apart: 4, of which 4 were waited for; matrix products, arithmetic and copies ran while one was open for 2% of the time, Pallas kernels for 0%

commit v1 on v0

v1 whole, which is shorter than its diff:
```python
import functools

import jax
import jax.numpy as jnp
from jax import lax
from jax.experimental import pallas as pl
from jax.experimental.pallas import tpu as pltpu
from jax.sharding import PartitionSpec as P

P_SIZE = 256
BLK = 32
LANES = 128
CORES = 2
EXTRA = 8
F32 = jnp.float32
BF16 = jnp.bfloat16


def split3(value):
    parts = []
    for _ in range(3):
        part = value.astype(BF16).astype(F32)
        parts.append(part)
        value = value - part
    return parts


def moment_kernel(tile, x_ref, panel_ref, wcol_ref, wrow_ref, out_ref, lhs, pcol, fixed):
    users = x_ref.shape[0]
    step = users // 4

    @pl.when(pl.program_id(0) == 0)
    def _():
        for r in range(0, users, step):
            rows = pl.ds(r, step)
            weighted = (wcol_ref[rows, :] * panel_ref[rows, :].astype(F32)).astype(BF16)
            lhs[0:P_SIZE, r : r + step] = weighted.T
        wrow = wrow_ref[...]
        lhs[P_SIZE:, :] = jnp.broadcast_to(wrow, (16, users))
        count = jnp.sum(wrow.astype(F32), axis=1, keepdims=True)
        total = jnp.dot(
            jnp.broadcast_to(wrow, (8, users)), panel_ref[...], preferred_element_type=F32
        )
        mean = total / count
        pcol[...] = jnp.concatenate([mean] * 16, axis=0).T
        hi, mid, lo = split3(mean[0:1])
        chi, cmid, clo = split3(jnp.broadcast_to(count, (1, LANES)))
        rows = [v[:, h : h + LANES] for v in (hi, mid, lo) for h in (0, LANES)]
        lane = lax.broadcasted_iota(jnp.int32, (1, LANES), 1)
        last = jnp.where(lane < 32, chi, jnp.where(lane < 64, cmid, clo))
        fixed[...] = jnp.concatenate(rows + [jnp.broadcast_to(count, (1, LANES)), last], axis=0)

    acc = jnp.dot(lhs[...], x_ref[...], preferred_element_type=F32)
    inverse = 1.0 / fixed[6:7, 0:1]
    mrow = acc[P_SIZE : P_SIZE + 1, :] * inverse
    moment = acc[0:P_SIZE, :] * inverse - pcol[:, 0:1] * mrow
    top = jnp.max(jnp.max(jnp.abs(moment), axis=0, keepdims=True), axis=1, keepdims=True)
    scale = (32768.0 / jnp.maximum(top, 1e-30)).astype(BF16).astype(F32)
    v = moment * scale
    v2 = v * v
    coded = (v * jnp.abs(v) * v2 * (v2 * v2)).astype(BF16).T
    pieces = tile // BLK
    coded = coded.reshape(pieces, BLK, P_SIZE)
    out_ref[:, 0:BLK, :] = coded[:, :, 0:LANES]
    out_ref[:, BLK : 2 * BLK, :] = coded[:, :, LANES:]

    hi, mid, lo = split3(mrow)
    lane = lax.broadcasted_iota(jnp.int32, (1, tile), 1) % LANES
    lane8 = lax.broadcasted_iota(jnp.int32, (EXTRA, LANES), 1)
    row8 = lax.broadcasted_iota(jnp.int32, (EXTRA, LANES), 0)
    base = jnp.where((row8 == 7) & (lane8 >= 96), scale, fixed[...])
    per = LANES // BLK
    for q in range(per):
        mix = jnp.where(
            lane < 32,
            pltpu.roll(hi, (tile - 32 * q) % tile, 1),
            jnp.where(
                lane < 64,
                pltpu.roll(mid, (tile + 32 - 32 * q) % tile, 1),
                pltpu.roll(lo, (tile + 64 - 32 * q) % tile, 1),
            ),
        )
        for g in range(tile // LANES):
            row = jnp.broadcast_to(mix[:, g * LANES : (g + 1) * LANES], (EXTRA, LANES))
            stats = jnp.where(row8 == 6, row, base).astype(BF16)
            out_ref[g * per + q, 2 * BLK :, :] = stats


def moments(x, panel, weights, pieces):
    users, items = x.shape
    tile = 512
    return pl.pallas_call(
        functools.partial(moment_kernel, tile),
        grid=(items // tile,),
        in_specs=[
            pl.BlockSpec((users, tile), lambda i: (0, i)),
            pl.BlockSpec((users, P_SIZE), lambda i: (0, 0)),
            pl.BlockSpec((users, 1), lambda i: (0, 0)),
            pl.BlockSpec((1, users), lambda i: (0, 0)),
        ],
        out_specs=pl.BlockSpec((tile // BLK, 2 * BLK + EXTRA, LANES), lambda i: (i, 0, 0)),
        out_shape=jax.ShapeDtypeStruct((pieces, 2 * BLK + EXTRA, LANES), BF16),
        scratch_shapes=[
            pltpu.VMEM((P_SIZE + 16, users), BF16),
            pltpu.VMEM((P_SIZE, LANES), F32),
            pltpu.VMEM((EXTRA, LANES), F32),
        ],
        compiler_params=pltpu.CompilerParams(
            vmem_limit_bytes=40 * 2**20, dimension_semantics=("arbitrary",)
        ),
        cost_estimate=pl.CostEstimate(
            flops=2 * users * items * P_SIZE, bytes_accessed=20 * 2**20, transcendentals=0
        ),
    )(x, panel, weights.astype(F32).reshape(-1, 1), weights.reshape(1, -1))


def merge_kernel(groups, cycles, in_ref, cov_ref, mean_ref):
    stats0 = in_ref[:, 0, 2 * BLK :, :].astype(F32)
    part = lambda row: jnp.concatenate([stats0[:, row, :], stats0[:, row + 1, :]], axis=1)
    panel = part(0) + part(2) + part(4)
    last = stats0[:, 7, :]
    count = last[:, 0:1] + last[:, 32:33] + last[:, 64:65]
    share = count / jnp.sum(count, axis=0, keepdims=True)
    panel_dev = panel - jnp.sum(share * panel, axis=0, keepdims=True)
    for i in range(cycles):
        stats = in_ref[:, i, 2 * BLK :, :].astype(F32)
        row = stats[:, 6, :]
        mean = row[:, 0:32] + row[:, 32:64] + row[:, 64:96]
        mean_all = jnp.sum(share * mean, axis=0, keepdims=True)
        mean_ref[i : i + 1, :] = mean_all
        left = jnp.broadcast_to(share, (groups, 32)) * (mean - mean_all)
        left = jnp.concatenate([left] * 4, axis=1).T
        back = share / stats[:, 7, 96:97]
        first = jnp.zeros((BLK, LANES), F32)
        second = jnp.zeros((BLK, LANES), F32)
        for u in range(groups):
            y = in_ref[u, i, 0 : 2 * BLK, :].astype(F32)
            size = jnp.exp2(jnp.log2(jnp.abs(y)) * 0.125)
            v = jnp.where(y < 0, -size, size) * back[u : u + 1, :]
            col = left[0:BLK, u : u + 1]
            first = first + v[0:BLK] + col * panel_dev[u : u + 1, 0:LANES]
            second = second + v[BLK:] + col * panel_dev[u : u + 1, LANES:]
        cov_ref[i, :, 0:LANES] = first
        cov_ref[i, :, LANES:] = second


def merge(pieces, groups, cycles):
    return pl.pallas_call(
        functools.partial(merge_kernel, groups, cycles),
        out_shape=[
            jax.ShapeDtypeStruct((cycles, BLK, P_SIZE), F32),
            jax.ShapeDtypeStruct((cycles, BLK), F32),
        ],
        in_specs=[pl.BlockSpec(memory_space=pltpu.VMEM)],
        out_specs=[pl.BlockSpec(memory_space=pltpu.VMEM)] * 2,
        compiler_params=pltpu.CompilerParams(vmem_limit_bytes=24 * 2**20),
        cost_estimate=pl.CostEstimate(
            flops=20 * 2**20, bytes_accessed=3 * 2**20, transcendentals=2 * 2**20
        ),
    )(pieces.reshape(groups, cycles, *pieces.shape[1:]))


def spread_panel(x, chosen):
    users, items = x.shape
    ring = lax.axis_size("items")
    chips = ring // CORES
    me = lax.axis_index("items")
    core, chip = me % CORES, me // CORES
    owner = chosen // (items // P_SIZE)
    start = chosen % (items // P_SIZE) * P_SIZE
    half = users // CORES
    own = lax.dynamic_slice(x, (core * half, start), (half, P_SIZE))
    other = lax.dynamic_slice(x, ((1 - core) * half, start), (half, P_SIZE))
    across = [(i, i ^ 1) for i in range(ring)]
    got = lax.ppermute(other, "items", across)
    mine = jnp.where(core == owner % CORES, own, got)

    def send_from(root):
        def branch(block):
            return tuple(
                lax.ppermute(
                    block,
                    "items",
                    [
                        (root * CORES + c, (root + d) % chips * CORES + c)
                        for c in range(CORES)
                    ],
                )
                for d in range(1, chips)
            )

        return branch

    moved = lax.switch(owner // CORES, [send_from(root) for root in range(chips)], mine)
    away = (chip - owner // CORES) % chips
    for d, block in enumerate(moved):
        mine = jnp.where(away == d + 1, block, mine)
    got = lax.ppermute(mine, "items", across)
    low = jnp.where(core == 0, mine, got)
    high = jnp.where(core == 0, got, mine)
    return jnp.concatenate([low, high], axis=0)


def per_device(interactions, user_weights, panel_index):
    groups, ring = lax.axis_size("users"), lax.axis_size("items")
    panel = spread_panel(interactions, panel_index[0])
    pieces = moments(interactions, panel, user_weights, groups * ring)
    moved = lax.all_to_all(pieces, ("users", "items"), 0, 0, tiled=True)
    return tuple(merge(moved, groups, ring))


def solution(mesh):
    return jax.shard_map(
        per_device,
        mesh=mesh,
        in_specs=(P("users", "items"), P("users"), P()),
        out_specs=(P(None, ("users", "items"), None), P(None, ("users", "items"))),
        check_vma=False,
    )
```

time: 747 us -> 98.1 us (0.13)
  waiting for transfers between devices: 358 us -> 18.9 us
  local copies, waits for them, and re-layouts: 127 us -> 1.46 us
  other arithmetic: 83.8 us -> 1.41 us
  loops' own time: 57.3 us -> 0.02 us
  blocking collectives: 72.7 us -> 45.4 us
  matrix products: 22.3 us -> 0 us
  Pallas kernels: 0 us -> 16.7 us
  between operations: 14.8 us -> 1.37 us
    all_gather x1 -> x0, waiting for transfers between devices: 295 us -> none  [combined_all(): pieces = jax.tree.map(lambda part: lax.all_gather(part, axis), value)]
    slice x11 -> x0, local copies, waits for them, and re-layouts: 107 us -> none  [the longest x6 102 us: combined_all(): tail = jax.tree.map(lambda part: part[1:], pieces)]
    add x30 -> x0, other arithmetic: 77.3 us -> none  [the longest x15 77.1 us: chan_combine(): moment_a + moment_b]
    another operation x1, loops' own time: 57.3 us -> 0.02 us  [spread_panel(): lax.switch(owner // CORES, [send_from(root) for root in range(chips)], mine)]
    psum x1 -> x0, waiting for transfers between devices: 53.9 us -> none  [from_root(): return lax.psum(block, axis)]
    all_to_all x0 -> x1, blocking collectives: none -> 45.4 us  [per_device(): moved = lax.all_to_all(pieces, ('users', 'items'), 0, 0, tiled=True)]
    all_gather x2 -> x0, blocking collectives: 38.3 us -> none  [combined_all(): pieces = jax.tree.map(lambda part: lax.all_gather(part, axis), value)]
    unnamed x1 -> x0, blocking collectives: 34.3 us -> none
  transfers between devices with their start and end apart: 4 -> 5, of which waited for: 4 -> 4; matrix products, arithmetic and copies ran while one was open for 2% -> 0% of each run, Pallas kernels for 0% -> 0%
where the time goes in v1:
time: 98.1 us; the launch traced here: 97.3 us
  blocking collectives  45.4 us (46%)
  waiting for transfers between devices  18.9 us (19%)
  Pallas kernels  16.7 us (17%)
  starting transfers between devices  12.1 us (12%)
  local copies, waits for them, and re-layouts  1.46 us (1%)
  other arithmetic  1.41 us (1%)
  between operations  1.37 us (1%)
    all_to_all x1, blocking collectives, per_device(): moved = lax.all_to_all(pieces, ('users', 'items'), 0, 0, tiled=True)  45.4 us
    ppermute x3, waiting for transfers between devices, branch(): lax.ppermute(block, 'items', [(root * CORES + c, (root + d) % chips * COR...  16.2 us
    pallas_call x1, Pallas kernels, moments(): pl.pallas_call(functools.partial(moment_kernel, tile), grid=(items // til...  13.2 us
    ppermute x3, starting transfers between devices, branch(): lax.ppermute(block, 'items', [(root * CORES + c, (root + d) % chips * COR...  9.27 us
    pallas_call x1, Pallas kernels, merge(): pl.pallas_call(functools.partial(merge_kernel, groups, cycles), out_shape...  3.49 us
  transfers between devices with their start and end apart: 5, of which 4 were waited for; matrix products, arithmetic and copies ran while one was open for 0% of the time, Pallas kernels for 0%

profile of v1, /device:TPU:1, one launch (start us, length us, event | category | flops | bytes accessed | tf_op | source)
XLA Modules:
  0.0 97.3 jit_solution(14497066054421469881)
XLA Ops:
  1.3 1.1 %dynamic_slice.7 = bf16[1024,256]{1,0:T(8,128)(2,1)S(1)} dynamic-slice(bf16[2048,4096]{1,0:T(8,128)(2,1)} %x_ref.1, s32[]{:T(128)S(6)} %select_n.92, s32[]{:T(128)S(6)} %select_n.91), dynamic_slice_sizes={1024,256} | dynamic-slice | bytes 1048580 | tf_op jit(solution)/shard_map/dynamic_slice | solution.py:173
  2.4 0.0 copy-start
  2.4 1.5 %collective-permute-start.12 = (bf16[1024,256]{1,0:T(8,128)(2,1)S(1)}, bf16[1024,256]{1,0:T(8,128)(2,1)S(1)}, u32[]{:S(2)}, u32[]{:S(2)}) collective-permute-start(bf16[1024,256]{1,0:T(8,128)(2,1)S(1)} %dynamic_slice.7), channel_id=1, source_target_pairs={{0,1},{1,0},{2,3},{3,2},{4,5},{5,4},{6,7},{7,6},{8,9},{9,8},{10,11... | collective-permute-start | bytes 1572872 | tf_op jit(solution)/shard_map/ppermute | solution.py:175
  3.9 1.5 %collective-permute-done.12 = bf16[1024,256]{1,0:T(8,128)(2,1)S(1)} collective-permute-done((bf16[1024,256]{1,0:T(8,128)(2,1)S(1)}, bf16[1024,256]{1,0:T(8,128)(2,1)S(1)}, u32[]{:S(2)}, u32[]{:S(2)}) %collective-permute-start.12) | collective-permute-done | bytes 524320 | tf_op jit(solution)/shard_map/ppermute | solution.py:175
  5.5 1.2 %dynamic-slice_select_fusion = bf16[1024,256]{1,0:T(8,128)(2,1)S(1)} fusion(bf16[1024,256]{1,0:T(8,128)(2,1)S(1)} %collective-permute-done.12, bf16[2048,4096]{1,0:T(8,128)(2,1)} %x_ref.1, s32[]{:T(128)S(6)} %select_n.89, s32[]{:T(128)S(6)} %select_n.91, pred[]{:T(512)S(6)} %eq.23), kind=kLoop, calls=%fused_computation.2 | loop fusion | flops 262144 | bytes 1572873 | tf_op jit(solution)/shard_map/jit(_where)/select_n | solution.py:176
  6.6 25.5 %conditional.1 = (bf16[1024,256]{1,0:T(8,128)(2,1)}, bf16[1024,256]{1,0:T(8,128)(2,1)}, bf16[1024,256]{1,0:T(8,128)(2,1)}) conditional(s32[]{:T(128)} %clamp.3, bf16[1024,256]{1,0:T(8,128)(2,1)S(1)} %dynamic-slice_select_fusion, bf16[1024,256]{1,0:T(8,128)(2,1)S(1)} %dynamic-slice_select_fusion, ...), branch_computations={%region_0.1_spmd, %region_1.2_spmd, %region_2.3_spmd, %region_3.4_... | conditional | bytes 6291600 | solution.py:194
  6.6 4.1 %collective-permute-start = (bf16[1024,256]{1,0:T(8,128)(2,1)S(1)}, bf16[1024,256]{1,0:T(8,128)(2,1)}, u32[]{:S(2)}, u32[]{:S(2)}) collective-permute-start(bf16[1024,256]{1,0:T(8,128)(2,1)S(1)} %param), channel_id=1, source_target_pairs={{0,2},{1,3},{8,10},{9,11},{16,18},{17,19},{24,26},{25,27},{32,34},... | collective-permute-start | bytes 1572872 | tf_op jit(solution)/shard_map/cond/branch_0_fun/ppermute | solution.py:181
  10.7 3.1 %collective-permute-start.1 = (bf16[1024,256]{1,0:T(8,128)(2,1)S(1)}, bf16[1024,256]{1,0:T(8,128)(2,1)}, u32[]{:S(2)}, u32[]{:S(2)}) collective-permute-start(bf16[1024,256]{1,0:T(8,128)(2,1)S(1)} %param), channel_id=1, source_target_pairs={{0,4},{1,5},{8,12},{9,13},{16,20},{17,21},{24,28},{25,29},{32,36},... | collective-permute-start | bytes 1572872 | tf_op jit(solution)/shard_map/cond/branch_0_fun/ppermute | solution.py:181
  13.8 2.1 %collective-permute-start.2 = (bf16[1024,256]{1,0:T(8,128)(2,1)S(1)}, bf16[1024,256]{1,0:T(8,128)(2,1)}, u32[]{:S(2)}, u32[]{:S(2)}) collective-permute-start(bf16[1024,256]{1,0:T(8,128)(2,1)S(1)} %param), channel_id=1, source_target_pairs={{0,6},{1,7},{8,14},{9,15},{16,22},{17,23},{24,30},{25,31},{32,38},... | collective-permute-start | bytes 1572872 | tf_op jit(solution)/shard_map/cond/branch_0_fun/ppermute | solution.py:181
  15.9 4.9 %collective-permute-done = bf16[1024,256]{1,0:T(8,128)(2,1)} collective-permute-done((bf16[1024,256]{1,0:T(8,128)(2,1)S(1)}, bf16[1024,256]{1,0:T(8,128)(2,1)}, u32[]{:S(2)}, u32[]{:S(2)}) %collective-permute-start) | collective-permute-done | bytes 524320 | tf_op jit(solution)/shard_map/cond/branch_0_fun/ppermute | solution.py:181
  20.8 11.2 %collective-permute-done.1 = bf16[1024,256]{1,0:T(8,128)(2,1)} collective-permute-done((bf16[1024,256]{1,0:T(8,128)(2,1)S(1)}, bf16[1024,256]{1,0:T(8,128)(2,1)}, u32[]{:S(2)}, u32[]{:S(2)}) %collective-permute-start.1) | collective-permute-done | bytes 524320 | tf_op jit(solution)/shard_map/cond/branch_0_fun/ppermute | solution.py:181
  32.1 0.0 collective-permute-done.2
  32.1 0.1 select_select_fusion
  32.2 1.3 %collective-permute-start.13 = (bf16[1024,256]{1,0:T(8,128)(2,1)S(1)}, bf16[1024,256]{1,0:T(8,128)(2,1)S(1)}, u32[]{:S(2)}, u32[]{:S(2)}) collective-permute-start(bf16[1024,256]{1,0:T(8,128)(2,1)S(1)} %select_select_fusion), channel_id=1, source_target_pairs={{0,1},{1,0},{2,3},{3,2},{4,5},{5,4},{6,7},{7,6},{8,9},{9,8},{10,11... | collective-permute-start | bytes 1572872 | tf_op jit(solution)/shard_map/ppermute | solution.py:198
  33.5 0.0 copy-done
  33.5 0.4 copy.5.wcol_ref
  33.9 1.1 %collective-permute-done.13 = bf16[1024,256]{1,0:T(8,128)(2,1)S(1)} collective-permute-done((bf16[1024,256]{1,0:T(8,128)(2,1)S(1)}, bf16[1024,256]{1,0:T(8,128)(2,1)S(1)}, u32[]{:S(2)}, u32[]{:S(2)}) %collective-permute-start.13) | collective-permute-done | bytes 524320 | tf_op jit(solution)/shard_map/ppermute | solution.py:198
  35.0 0.1 broadcast_select_fusion.1
  35.1 0.1 pad_maximum_fusion.panel_ref
  35.2 13.2 %shard_map.50 = bf16[128,72,128]{2,1,0:T(8,128)(2,1)S(1)} custom-call(bf16[2048,4096]{1,0:T(8,128)(2,1)} %x_ref.1, bf16[2048,256]{1,0:T(8,128)(2,1)S(1)} %pad_maximum_fusion.panel_ref, f32[2048,1]{1,0:T(8,128)S(1)} %copy.5.wcol_ref, bf16[1,2048]{1,0:T(2,128)(2,1)S(1)} %reshape.17.wrow_ref), custom_call_target="tpu_custom_call" | custom-call | flops 4294967296 | bytes 20971520 | tf_op jit(solution)/shard_map/pallas_call | solution.py:92
  48.4 45.4 %all_to_all.5 = bf16[128,72,128]{2,1,0:T(8,128)(2,1)S(1)} all-to-all(bf16[128,72,128]{2,1,0:T(8,128)(2,1)S(1)} %shard_map.50), channel_id=1, replica_groups=mesh['users'=16,'items'=8] {'users','items'}, dimensions={0} | all-to-all | bytes 4718592 | tf_op jit(solution)/shard_map/all_to_all | solution.py:208
  93.8 3.5 %shard_map.51 = (f32[8,32,256]{2,1,0:T(8,128)}, f32[8,32]{1,0:T(8,128)}) custom-call(bf16[16,8,72,128]{3,2,1,0:T(8,128)(2,1)S(1)} %bitcast.7), custom_call_target="tpu_custom_call" | custom-call | flops 20971520 | bytes 3145728 | tf_op jit(solution)/shard_map/pallas_call | solution.py:148
  (2 shorter events, 0.0 us)
Async XLA Ops:
  2.4 31.1 %copy-start = (bf16[2048]{0:T(1024)(128)(2,1)S(1)}, bf16[2048]{0:T(1024)(128)(2,1)}, u32[]{:S(2)}) copy-start(bf16[2048]{0:T(1024)(128)(2,1)} %param.8) | copy-start | bytes 12292
  2.4 3.0 %collective-permute-start.12 = (bf16[1024,256]{1,0:T(8,128)(2,1)S(1)}, bf16[1024,256]{1,0:T(8,128)(2,1)S(1)}, u32[]{:S(2)}, u32[]{:S(2)}) collective-permute-start(bf16[1024,256]{1,0:T(8,128)(2,1)S(1)} %dynamic_slice.7), channel_id=1, source_target_pairs={{0,1},{1,0},{2,3},{3,2},{4,5},{5,4},{6,7},{7,6},{8,9},{9,8},{10,11... | collective-permute-start | bytes 1572872 | tf_op jit(solution)/shard_map/ppermute | solution.py:175
  6.6 14.2 %collective-permute-start = (bf16[1024,256]{1,0:T(8,128)(2,1)S(1)}, bf16[1024,256]{1,0:T(8,128)(2,1)}, u32[]{:S(2)}, u32[]{:S(2)}) collective-permute-start(bf16[1024,256]{1,0:T(8,128)(2,1)S(1)} %param), channel_id=1, source_target_pairs={{0,2},{1,3},{8,10},{9,11},{16,18},{17,19},{24,26},{25,27},{32,34},... | collective-permute-start | bytes 1572872 | tf_op jit(solution)/shard_map/cond/branch_0_fun/ppermute | solution.py:181
  10.7 21.4 %collective-permute-start.1 = (bf16[1024,256]{1,0:T(8,128)(2,1)S(1)}, bf16[1024,256]{1,0:T(8,128)(2,1)}, u32[]{:S(2)}, u32[]{:S(2)}) collective-permute-start(bf16[1024,256]{1,0:T(8,128)(2,1)S(1)} %param), channel_id=1, source_target_pairs={{0,4},{1,5},{8,12},{9,13},{16,20},{17,21},{24,28},{25,29},{32,36},... | collective-permute-start | bytes 1572872 | tf_op jit(solution)/shard_map/cond/branch_0_fun/ppermute | solution.py:181
  13.8 18.3 %collective-permute-start.2 = (bf16[1024,256]{1,0:T(8,128)(2,1)S(1)}, bf16[1024,256]{1,0:T(8,128)(2,1)}, u32[]{:S(2)}, u32[]{:S(2)}) collective-permute-start(bf16[1024,256]{1,0:T(8,128)(2,1)S(1)} %param), channel_id=1, source_target_pairs={{0,6},{1,7},{8,14},{9,15},{16,22},{17,23},{24,30},{25,31},{32,38},... | collective-permute-start | bytes 1572872 | tf_op jit(solution)/shard_map/cond/branch_0_fun/ppermute | solution.py:181
  32.2 2.8 %collective-permute-start.13 = (bf16[1024,256]{1,0:T(8,128)(2,1)S(1)}, bf16[1024,256]{1,0:T(8,128)(2,1)S(1)}, u32[]{:S(2)}, u32[]{:S(2)}) collective-permute-start(bf16[1024,256]{1,0:T(8,128)(2,1)S(1)} %select_select_fusion), channel_id=1, source_target_pairs={{0,1},{1,0},{2,3},{3,2},{4,5},{5,4},{6,7},{7,6},{8,9},{9,8},{10,11... | collective-permute-start | bytes 1572872 | tf_op jit(solution)/shard_map/ppermute | solution.py:198

commit v2 on v1

v2 whole, which is shorter than its diff:
```python
import functools

import jax
import jax.numpy as jnp
from jax import lax
from jax.experimental import pallas as pl
from jax.experimental.pallas import tpu as pltpu
from jax.sharding import PartitionSpec as P

P_SIZE = 256
BLK = 32
LANES = 128
CORES = 2
CORE, AWAY, SAME = range(3)
EXTRA = 8
F32 = jnp.float32
BF16 = jnp.bfloat16


def split3(value):
    parts = []
    for _ in range(3):
        part = value.astype(BF16).astype(F32)
        parts.append(part)
        value = value - part
    return parts


def touch_kernel(x_ref, after_ref, out_ref):
    out_ref[...] = jnp.zeros_like(out_ref)


def touch(x, after):
    return pl.pallas_call(
        touch_kernel,
        in_specs=[pl.BlockSpec(memory_space=pltpu.VMEM), pl.BlockSpec(memory_space=pl.ANY)],
        out_specs=pl.BlockSpec(memory_space=pltpu.VMEM),
        out_shape=jax.ShapeDtypeStruct((8, LANES), F32),
        compiler_params=pltpu.CompilerParams(vmem_limit_bytes=2 * 2**20),
        cost_estimate=pl.CostEstimate(
            flops=0, bytes_accessed=x.size * x.dtype.itemsize, transcendentals=0
        ),
    )(x, after)


def turn_kernel(right_ref, left_ref, after_ref, first_ref, second_ref):
    part = first_ref.shape[0]
    first_ref[...] = right_ref[0:part, :]
    second_ref[...] = left_ref[part:, :]


def turn(right, left, after):
    rows, columns = right.shape
    shape = jax.ShapeDtypeStruct((rows // 2, columns), right.dtype)
    return pl.pallas_call(
        turn_kernel,
        in_specs=[pl.BlockSpec(memory_space=pltpu.VMEM)] * 2 + [pl.BlockSpec(memory_space=pl.ANY)],
        out_specs=[pl.BlockSpec(memory_space=pltpu.VMEM)] * 2,
        out_shape=[shape, shape],
        compiler_params=pltpu.CompilerParams(vmem_limit_bytes=4 * 2**20),
        cost_estimate=pl.CostEstimate(flops=0, bytes_accessed=2**20, transcendentals=0),
    )(right, left, after)


def choose_kernel(info_ref, own_ref, got_ref, out_ref):
    @pl.when(info_ref[SAME] == 1)
    def _():
        out_ref[...] = own_ref[...]

    @pl.when(info_ref[SAME] != 1)
    def _():
        out_ref[...] = got_ref[...]


def join_kernel(info_ref, mine_ref, right_ref, left_ref, far_a_ref, far_b_ref, out_ref):
    part = far_a_ref.shape[0]
    for k, ref in ((0, mine_ref), (1, right_ref), (3, left_ref)):

        @pl.when(info_ref[AWAY] == k)
        def _():
            out_ref[...] = ref[...]

    @pl.when(info_ref[AWAY] == 2)
    def _():
        out_ref[0:part, :] = far_a_ref[...]
        out_ref[part:, :] = far_b_ref[...]


def select(kernel, info, *blocks):
    return pl.pallas_call(
        kernel,
        in_specs=[pl.BlockSpec(memory_space=pltpu.SMEM)]
        + [pl.BlockSpec(memory_space=pltpu.VMEM)] * len(blocks),
        out_specs=pl.BlockSpec(memory_space=pltpu.VMEM),
        out_shape=jax.ShapeDtypeStruct(blocks[0].shape, blocks[0].dtype),
        compiler_params=pltpu.CompilerParams(vmem_limit_bytes=2 * 2**20),
        cost_estimate=pl.CostEstimate(flops=0, bytes_accessed=2**20, transcendentals=0),
    )(info, *blocks)


def moment_kernel(tile, info_ref, w_ref, mine_ref, other_ref, x_ref, out_ref, lhs):
    users, items = x_ref.shape
    half = users // CORES
    lanes16 = w_ref[...]
    wrow = jnp.concatenate([lanes16[k : k + 1, :] for k in range(users // LANES)], axis=1)
    wrow32 = wrow.astype(F32)
    count = jnp.sum(wrow32, axis=1, keepdims=True)
    total = jnp.zeros((P_SIZE, LANES), F32)
    first = info_ref[CORE] == 0
    low = jnp.where(first, mine_ref[...], other_ref[...])
    high = jnp.where(first, other_ref[...], mine_ref[...])
    for k, part in enumerate((low, high)):
        cut = slice(k * half, (k + 1) * half)
        product = part.T.astype(F32) * wrow32[:, cut]
        lhs[0:P_SIZE, cut] = product.astype(BF16)
        for g in range(0, half, LANES):
            total += product[:, g : g + LANES]
    lhs[P_SIZE:, :] = jnp.broadcast_to(wrow, (16, users))
    inverse = 1.0 / count
    pcol = jnp.sum(total, axis=1, keepdims=True) * inverse
    prow = jnp.broadcast_to(pcol, (P_SIZE, LANES)).T[0:1, :]
    hi, mid, lo = split3(prow)
    chi, cmid, clo = split3(jnp.broadcast_to(count, (1, LANES)))
    rows = [v[:, h : h + LANES] for v in (hi, mid, lo) for h in (0, LANES)]
    lane1 = lax.broadcasted_iota(jnp.int32, (1, LANES), 1)
    last = jnp.where(lane1 < 32, chi, jnp.where(lane1 < 64, cmid, clo))
    fixed = jnp.concatenate(rows + [last, last], axis=0)
    lane = lax.broadcasted_iota(jnp.int32, (1, tile), 1) % LANES
    lane8 = lax.broadcasted_iota(jnp.int32, (EXTRA, LANES), 1)
    row8 = lax.broadcasted_iota(jnp.int32, (EXTRA, LANES), 0)
    per = LANES // BLK
    pieces = tile // BLK

    for t in range(items // tile):
        acc = jnp.dot(
            lhs[...], x_ref[:, t * tile : (t + 1) * tile], preferred_element_type=F32
        )
        mrow = acc[P_SIZE : P_SIZE + 1, :] * inverse
        moment = acc[0:P_SIZE, :] * inverse - pcol * mrow
        top = jnp.max(jnp.max(jnp.abs(moment), axis=0, keepdims=True), axis=1, keepdims=True)
        scale = (32768.0 / jnp.maximum(top, 1e-30)).astype(BF16).astype(F32)
        v = moment * scale
        v2 = v * v
        coded = (v * jnp.abs(v) * v2 * (v2 * v2)).astype(BF16).T.reshape(pieces, BLK, P_SIZE)
        place = slice(t * pieces, (t + 1) * pieces)
        out_ref[place, 0:BLK, :] = coded[:, :, 0:LANES]
        out_ref[place, BLK : 2 * BLK, :] = coded[:, :, LANES:]
        hi, mid, lo = split3(mrow)
        base = jnp.where((row8 == 7) & (lane8 >= 96), scale, fixed)
        for q in range(per):
            mix = jnp.where(
                lane < 32,
                pltpu.roll(hi, (tile - 32 * q) % tile, 1),
                jnp.where(
                    lane < 64,
                    pltpu.roll(mid, (tile + 32 - 32 * q) % tile, 1),
                    pltpu.roll(lo, (tile + 64 - 32 * q) % tile, 1),
                ),
            )
            for g in range(tile // LANES):
                row = jnp.broadcast_to(mix[:, g * LANES : (g + 1) * LANES], (EXTRA, LANES))
                stats = jnp.where(row8 == 6, row, base).astype(BF16)
                out_ref[t * pieces + g * per + q, 2 * BLK :, :] = stats


def moments(info, x, mine, other, weights, pieces):
    users, items = x.shape
    tile = 512
    return pl.pallas_call(
        functools.partial(moment_kernel, tile),
        in_specs=[pl.BlockSpec(memory_space=pltpu.SMEM)]
        + [pl.BlockSpec(memory_space=pltpu.VMEM)] * 4,
        out_specs=pl.BlockSpec(memory_space=pltpu.VMEM),
        out_shape=jax.ShapeDtypeStruct((pieces, 2 * BLK + EXTRA, LANES), BF16),
        scratch_shapes=[pltpu.VMEM((P_SIZE + 16, users), BF16)],
        compiler_params=pltpu.CompilerParams(vmem_limit_bytes=16 * 2**20),
        cost_estimate=pl.CostEstimate(
            flops=2 * users * items * P_SIZE, bytes_accessed=4 * 2**20, transcendentals=0
        ),
    )(info, weights.reshape(-1, LANES), mine, other, x)


def merge_kernel(groups, cycles, in_ref, cov_ref, mean_ref):
    stats0 = in_ref[:, 0, 2 * BLK :, :].astype(F32)
    part = lambda row: jnp.concatenate([stats0[:, row, :], stats0[:, row + 1, :]], axis=1)
    panel = part(0) + part(2) + part(4)
    last = stats0[:, 7, :]
    count = last[:, 0:1] + last[:, 32:33] + last[:, 64:65]
    share = count / jnp.sum(count, axis=0, keepdims=True)
    panel_dev = panel - jnp.sum(share * panel, axis=0, keepdims=True)
    for i in range(cycles):
        stats = in_ref[:, i, 2 * BLK :, :].astype(F32)
        row = stats[:, 6, :]
        mean = row[:, 0:32] + row[:, 32:64] + row[:, 64:96]
        mean_all = jnp.sum(share * mean, axis=0, keepdims=True)
        mean_ref[i : i + 1, :] = mean_all
        left = jnp.broadcast_to(share, (groups, 32)) * (mean - mean_all)
        left = jnp.concatenate([left] * 4, axis=1).T
        back = share / stats[:, 7, 96:97]
        first = jnp.zeros((BLK, LANES), F32)
        second = jnp.zeros((BLK, LANES), F32)
        for u in range(groups):
            y = in_ref[u, i, 0 : 2 * BLK, :].astype(F32)
            size = jnp.exp2(jnp.log2(jnp.abs(y)) * 0.125)
            v = jnp.where(y < 0, -size, size) * back[u : u + 1, :]
            col = left[0:BLK, u : u + 1]
            first = first + v[0:BLK] + col * panel_dev[u : u + 1, 0:LANES]
            second = second + v[BLK:] + col * panel_dev[u : u + 1, LANES:]
        cov_ref[i, :, 0:LANES] = first
        cov_ref[i, :, LANES:] = second


def merge(pieces, groups, cycles):
    return pl.pallas_call(
        functools.partial(merge_kernel, groups, cycles),
        out_shape=[
            jax.ShapeDtypeStruct((cycles, BLK, P_SIZE), F32),
            jax.ShapeDtypeStruct((cycles, BLK), F32),
        ],
        in_specs=[pl.BlockSpec(memory_space=pltpu.VMEM)],
        out_specs=[pl.BlockSpec(memory_space=pltpu.VMEM)] * 2,
        compiler_params=pltpu.CompilerParams(vmem_limit_bytes=24 * 2**20),
        cost_estimate=pl.CostEstimate(
            flops=20 * 2**20, bytes_accessed=3 * 2**20, transcendentals=2 * 2**20
        ),
    )(pieces.reshape(groups, cycles, *pieces.shape[1:]))


def spread_panel(x, info, core, start):
    ring = lax.axis_size("items")
    chips = ring // CORES
    half = x.shape[0] // CORES
    across = [(i, i ^ 1) for i in range(ring)]

    def step(block, distance):
        pairs = [
            (y * CORES + c, (y + distance) % chips * CORES + c)
            for y in range(chips)
            for c in range(CORES)
        ]
        return lax.ppermute(block, "items", pairs)

    own = lax.dynamic_slice(x, (core * half, start), (half, P_SIZE))
    other = lax.dynamic_slice(x, ((1 - core) * half, start), (half, P_SIZE))
    mine = select(choose_kernel, info, own, lax.ppermute(other, "items", across))
    right, left = step(mine, 1), step(mine, -1)
    first, second = turn(right, left, touch(x, mine))
    far_a, far_b = step(first, 1), step(second, -1)
    mine = select(join_kernel, info, mine, right, left, far_a, far_b)
    return mine, lax.ppermute(mine, "items", across)


def per_device(interactions, user_weights, panel_index):
    groups, ring = lax.axis_size("users"), lax.axis_size("items")
    me, chips = lax.axis_index("items"), ring // CORES
    per_shard = interactions.shape[1] // P_SIZE
    owner, place = panel_index[0] // per_shard, panel_index[0] % per_shard
    core = me % CORES
    away = (me // CORES - owner // CORES) % chips
    same = (core == owner % CORES).astype(jnp.int32)
    info = jnp.stack([core, away, same]).astype(jnp.int32)
    mine, other = spread_panel(interactions, info, core, place * P_SIZE)
    pieces = moments(info, interactions, mine, other, user_weights, groups * ring)
    moved = lax.all_to_all(pieces, ("users", "items"), 0, 0, tiled=True)
    return tuple(merge(moved, groups, ring))


def solution(mesh):
    return jax.shard_map(
        per_device,
        mesh=mesh,
        in_specs=(P("users", "items"), P("users"), P()),
        out_specs=(P(None, ("users", "items"), None), P(None, ("users", "items"))),
        check_vma=False,
    )
```

time: 98.1 us -> 89.8 us (0.915)
  local copies, waits for them, and re-layouts: 1.46 us -> 7.06 us
  Pallas kernels: 16.7 us -> 12.1 us
  waiting for transfers between devices: 18.9 us -> 16.1 us
  starting transfers between devices: 12.1 us -> 9.65 us
  blocking collectives: 45.4 us -> 43.2 us
  other arithmetic: 1.41 us -> 0.08 us
    unnamed x2 -> x6, local copies, waits for them, and re-layouts: 0.01 us -> 5.78 us
    pallas_call x1 -> x5, Pallas kernels: 13.2 us -> 8.64 us  [the longest x1 7.41 us: moments(): pl.pallas_call(functools.partial(moment_kernel, tile), in_specs=[pl.Block...]
    ppermute x5 -> x6, waiting for transfers between devices: 18.9 us -> 16.1 us  [the longest x4 13.1 us: step(): return lax.ppermute(block, 'items', pairs)]
    ppermute x5 -> x6, starting transfers between devices: 12.1 us -> 9.65 us  [the longest x4 5.63 us: step(): return lax.ppermute(block, 'items', pairs)]
    all_to_all x1, blocking collectives: 45.4 us -> 43.2 us  [per_device(): moved = lax.all_to_all(pieces, ('users', 'items'), 0, 0, tiled=True)]
    select_n x3 -> x0, other arithmetic: 1.33 us -> none  [the longest x1 1.16 us: spread_panel(): mine = jnp.where(core == owner % CORES, own, got)]
  transfers between devices with their start and end apart: 5 -> 6, of which waited for: 4 -> 5; matrix products, arithmetic and copies ran while one was open for 0% -> 0% of each run, Pallas kernels for 0% -> 0%
where the time goes in v2:
time: 89.8 us; the launch traced here: 89.6 us
  blocking collectives  43.2 us (48%)
  waiting for transfers between devices  16.1 us (18%)
  Pallas kernels  12.1 us (13%)
  starting transfers between devices  9.65 us (11%)
  local copies, waits for them, and re-layouts  7.06 us (8%)
  between operations  1.37 us (2%)
    all_to_all x1, blocking collectives, per_device(): moved = lax.all_to_all(pieces, ('users', 'items'), 0, 0, tiled=True)  43.2 us
    ppermute x4, waiting for transfers between devices, step(): return lax.ppermute(block, 'items', pairs)  13.1 us
    pallas_call x1, Pallas kernels, moments(): pl.pallas_call(functools.partial(moment_kernel, tile), in_specs=[pl.Block...  7.41 us
    unnamed x6, local copies, waits for them, and re-layouts  5.78 us
    ppermute x4, starting transfers between devices, step(): return lax.ppermute(block, 'items', pairs)  5.63 us
    pallas_call x1, Pallas kernels, merge(): pl.pallas_call(functools.partial(merge_kernel, groups, cycles), out_shape...  3.49 us
    ppermute x1, starting transfers between devices, spread_panel(): return (mine, lax.ppermute(mine, 'items', across))  2.53 us
  transfers between devices with their start and end apart: 6, of which 5 were waited for; matrix products, arithmetic and copies ran while one was open for 0% of the time, Pallas kernels for 0%

profile of v2, /device:TPU:1, one launch (start us, length us, event | category | flops | bytes accessed | tf_op | source)
XLA Modules:
  0.0 89.6 jit_solution(3832689715060845229)
XLA Ops:
  0.6 0.0 copy-start.2
  1.3 1.3 %fusion = (bf16[1024,256]{1,0:T(8,128)(2,1)S(1)}, bf16[1024,256]{1,0:T(8,128)(2,1)S(1)}) fusion(bf16[2048,4096]{1,0:T(8,128)(2,1)} %x_ref.3, s32[]{:T(128)S(6)} %select_n.48, s32[]{:T(128)S(6)} %select_n.47, s32[]{:T(128)S(6)} %select_n.45), kind=kLoop, calls=%fused_computation.1 | loop fusion | bytes 2097164 | tf_op jit(solution)/shard_map/dynamic_slice | solution.py:244
  2.6 1.5 %collective-permute-start = (bf16[1024,256]{1,0:T(8,128)(2,1)S(1)}, bf16[1024,256]{1,0:T(8,128)(2,1)S(1)}, u32[]{:S(2)}, u32[]{:S(2)}) collective-permute-start(bf16[1024,256]{1,0:T(8,128)(2,1)S(1)} %get-tuple-element.6), channel_id=1, source_target_pairs={{0,1},{1,0},{2,3},{3,2},{4,5},{5,4},{6,7},{7,6},{8,9},{9,8},{10,11... | collective-permute-start | bytes 1572872 | tf_op jit(solution)/shard_map/ppermute | solution.py:245
  4.1 0.1 pad_add_fusion.info_ref
  4.2 1.5 %collective-permute-done.got_ref = bf16[1024,256]{1,0:T(8,128)(2,1)S(1)} collective-permute-done((bf16[1024,256]{1,0:T(8,128)(2,1)S(1)}, bf16[1024,256]{1,0:T(8,128)(2,1)S(1)}, u32[]{:S(2)}, u32[]{:S(2)}) %collective-permute-start) | collective-permute-done | bytes 524320 | tf_op jit(solution)/shard_map/ppermute | solution.py:245
  5.7 0.6 shard_map.50.after_ref.mine_ref
  6.3 2.9 %collective-permute-start.2 = (bf16[1024,256]{1,0:T(8,128)(2,1)S(1)}, bf16[1024,256]{1,0:T(8,128)(2,1)S(1)}, u32[]{:S(2)}, u32[]{:S(2)}) collective-permute-start(bf16[1024,256]{1,0:T(8,128)(2,1)S(1)} %shard_map.50.after_ref.mine_ref), channel_id=1, source_target_pairs={{0,6},{1,7},{2,0},{3,1},{4,2},{5,3},{6,4},{7,5},{8,14},{9,15},{10,... | collective-permute-start | bytes 1572872 | tf_op jit(solution)/shard_map/ppermute | solution.py:241
  9.1 0.0 collective-permute-start.1
  9.1 0.0 copy-start
  9.1 5.8 %copy-done = bf16[2048,4096]{1,0:T(8,128)(2,1)S(1)} copy-done((bf16[2048,4096]{1,0:T(8,128)(2,1)S(1)}, bf16[2048,4096]{1,0:T(8,128)(2,1)}, u32[]{:S(2)}) %copy-start) | copy-done | bytes 16777240
  14.9 0.0 copy-start.1
  14.9 5.2 %collective-permute-done.2.left_ref = bf16[1024,256]{1,0:T(8,128)(2,1)S(1)} collective-permute-done((bf16[1024,256]{1,0:T(8,128)(2,1)S(1)}, bf16[1024,256]{1,0:T(8,128)(2,1)S(1)}, u32[]{:S(2)}, u32[]{:S(2)}) %collective-permute-start.2) | collective-permute-done | bytes 524320 | tf_op jit(solution)/shard_map/ppermute | solution.py:241
  20.1 3.1 %collective-permute-done.1.right_ref = bf16[1024,256]{1,0:T(8,128)(2,1)S(1)} collective-permute-done((bf16[1024,256]{1,0:T(8,128)(2,1)S(1)}, bf16[1024,256]{1,0:T(8,128)(2,1)S(1)}, u32[]{:S(2)}, u32[]{:S(2)}) %collective-permute-start.1) | collective-permute-done | bytes 524320 | tf_op jit(solution)/shard_map/ppermute | solution.py:241
  23.2 0.1 collective-permute-start.3
  23.3 2.7 %collective-permute-start.4 = (bf16[512,256]{1,0:T(8,128)(2,1)S(1)}, bf16[512,256]{1,0:T(8,128)(2,1)S(1)}, u32[]{:S(2)}, u32[]{:S(2)}) collective-permute-start(bf16[512,256]{1,0:T(8,128)(2,1)S(1)} %get-tuple-element.5), channel_id=1, source_target_pairs={{0,6},{1,7},{2,0},{3,1},{4,2},{5,3},{6,4},{7,5},{8,14},{9,15},{10,... | collective-permute-start | bytes 786440 | tf_op jit(solution)/shard_map/ppermute | solution.py:241
  25.9 4.8 %collective-permute-done.3.far_a_ref = bf16[512,256]{1,0:T(8,128)(2,1)S(1)} collective-permute-done((bf16[512,256]{1,0:T(8,128)(2,1)S(1)}, bf16[512,256]{1,0:T(8,128)(2,1)S(1)}, u32[]{:S(2)}, u32[]{:S(2)}) %collective-permute-start.3) | collective-permute-done | bytes 262176 | tf_op jit(solution)/shard_map/ppermute | solution.py:241
  30.8 0.0 collective-permute-done.4.far_b_ref
  30.8 0.6 shard_map.53.mine_ref
  31.4 2.5 %collective-permute-start.5 = (bf16[1024,256]{1,0:T(8,128)(2,1)S(1)}, bf16[1024,256]{1,0:T(8,128)(2,1)S(1)}, u32[]{:S(2)}, u32[]{:S(2)}) collective-permute-start(bf16[1024,256]{1,0:T(8,128)(2,1)S(1)} %shard_map.53.mine_ref), channel_id=1, source_target_pairs={{0,1},{1,0},{2,3},{3,2},{4,5},{5,4},{6,7},{7,6},{8,9},{9,8},{10,11... | collective-permute-start | bytes 1572872 | tf_op jit(solution)/shard_map/ppermute | solution.py:250
  33.9 1.5 %collective-permute-done.5.other_ref = bf16[1024,256]{1,0:T(8,128)(2,1)S(1)} collective-permute-done((bf16[1024,256]{1,0:T(8,128)(2,1)S(1)}, bf16[1024,256]{1,0:T(8,128)(2,1)S(1)}, u32[]{:S(2)}, u32[]{:S(2)}) %collective-permute-start.5) | collective-permute-done | bytes 524320 | tf_op jit(solution)/shard_map/ppermute | solution.py:250
  35.4 0.0 copy-done.2
  35.4 0.0 copy-done.1
  35.4 7.4 %shard_map.54 = bf16[128,72,128]{2,1,0:T(8,128)(2,1)S(1)} custom-call(s32[3]{0:T(128)S(1)} %pad_add_fusion.info_ref, bf16[16,128]{1,0:T(8,128)(2,1)S(1)} %bitcast.11, bf16[1024,256]{1,0:T(8,128)(2,1)S(1)} %shard_map.53.mine_ref, bf16[1024,256]{1,0:T(8,128)(2,1)S(1)} %collective-permute-done.5.other_ref, bf16[2048,4096]{1,0:T(8,128)(2,1)S(1)} %copy-done.1), custom_call_target="tpu_custom_call" | custom-call | flops 4294967296 | bytes 4194304 | tf_op jit(solution)/shard_map/pallas_call | solution.py:169
  42.9 43.2 %all_to_all.5 = bf16[128,72,128]{2,1,0:T(8,128)(2,1)S(1)} all-to-all(bf16[128,72,128]{2,1,0:T(8,128)(2,1)S(1)} %shard_map.54), channel_id=1, replica_groups=mesh['users'=16,'items'=8] {'users','items'}, dimensions={0} | all-to-all | bytes 4718592 | tf_op jit(solution)/shard_map/all_to_all | solution.py:264
  86.1 3.5 %shard_map.55 = (f32[8,32,256]{2,1,0:T(8,128)}, f32[8,32]{1,0:T(8,128)}) custom-call(bf16[16,8,72,128]{3,2,1,0:T(8,128)(2,1)S(1)} %bitcast.10), custom_call_target="tpu_custom_call" | custom-call | flops 20971520 | bytes 3145728 | tf_op jit(solution)/shard_map/pallas_call | solution.py:214
  (2 shorter events, 0.0 us)
Async XLA Ops:
  0.6 34.8 %copy-start.2 = (bf16[2048]{0:T(1024)(128)(2,1)S(1)}, bf16[2048]{0:T(1024)(128)(2,1)}, u32[]{:S(2)}) copy-start(bf16[2048]{0:T(1024)(128)(2,1)} %param.4) | copy-start | bytes 12292
  2.6 3.0 %collective-permute-start = (bf16[1024,256]{1,0:T(8,128)(2,1)S(1)}, bf16[1024,256]{1,0:T(8,128)(2,1)S(1)}, u32[]{:S(2)}, u32[]{:S(2)}) collective-permute-start(bf16[1024,256]{1,0:T(8,128)(2,1)S(1)} %get-tuple-element.6), channel_id=1, source_target_pairs={{0,1},{1,0},{2,3},{3,2},{4,5},{5,4},{6,7},{7,6},{8,9},{9,8},{10,11... | collective-permute-start | bytes 1572872 | tf_op jit(solution)/shard_map/ppermute | solution.py:245
  6.3 13.8 %collective-permute-start.2 = (bf16[1024,256]{1,0:T(8,128)(2,1)S(1)}, bf16[1024,256]{1,0:T(8,128)(2,1)S(1)}, u32[]{:S(2)}, u32[]{:S(2)}) collective-permute-start(bf16[1024,256]{1,0:T(8,128)(2,1)S(1)} %shard_map.50.after_ref.mine_ref), channel_id=1, source_target_pairs={{0,6},{1,7},{2,0},{3,1},{4,2},{5,3},{6,4},{7,5},{8,14},{9,15},{10,... | collective-permute-start | bytes 1572872 | tf_op jit(solution)/shard_map/ppermute | solution.py:241
  9.1 14.0 %collective-permute-start.1 = (bf16[1024,256]{1,0:T(8,128)(2,1)S(1)}, bf16[1024,256]{1,0:T(8,128)(2,1)S(1)}, u32[]{:S(2)}, u32[]{:S(2)}) collective-permute-start(bf16[1024,256]{1,0:T(8,128)(2,1)S(1)} %shard_map.50.after_ref.mine_ref), channel_id=1, source_target_pairs={{0,2},{1,3},{2,4},{3,5},{4,6},{5,7},{6,0},{7,1},{8,10},{9,11},{10,... | collective-permute-start | bytes 1572872 | tf_op jit(solution)/shard_map/ppermute | solution.py:241
  9.1 5.8 %copy-start = (bf16[2048,4096]{1,0:T(8,128)(2,1)S(1)}, bf16[2048,4096]{1,0:T(8,128)(2,1)}, u32[]{:S(2)}) copy-start(bf16[2048,4096]{1,0:T(8,128)(2,1)} %x_ref.3) | copy-start | bytes 50331652
  14.9 20.5 %copy-start.1 = (bf16[2048,4096]{1,0:T(8,128)(2,1)S(1)}, bf16[2048,4096]{1,0:T(8,128)(2,1)}, u32[]{:S(2)}) copy-start(bf16[2048,4096]{1,0:T(8,128)(2,1)} %x_ref.3) | copy-start | bytes 50331652
  23.2 7.6 %collective-permute-start.3 = (bf16[512,256]{1,0:T(8,128)(2,1)S(1)}, bf16[512,256]{1,0:T(8,128)(2,1)S(1)}, u32[]{:S(2)}, u32[]{:S(2)}) collective-permute-start(bf16[512,256]{1,0:T(8,128)(2,1)S(1)} %get-tuple-element.4), channel_id=1, source_target_pairs={{0,2},{1,3},{2,4},{3,5},{4,6},{5,7},{6,0},{7,1},{8,10},{9,11},{10,... | collective-permute-start | bytes 786440 | tf_op jit(solution)/shard_map/ppermute | solution.py:241
  23.3 7.5 %collective-permute-start.4 = (bf16[512,256]{1,0:T(8,128)(2,1)S(1)}, bf16[512,256]{1,0:T(8,128)(2,1)S(1)}, u32[]{:S(2)}, u32[]{:S(2)}) collective-permute-start(bf16[512,256]{1,0:T(8,128)(2,1)S(1)} %get-tuple-element.5), channel_id=1, source_target_pairs={{0,6},{1,7},{2,0},{3,1},{4,2},{5,3},{6,4},{7,5},{8,14},{9,15},{10,... | collective-permute-start | bytes 786440 | tf_op jit(solution)/shard_map/ppermute | solution.py:241
  31.4 4.1 %collective-permute-start.5 = (bf16[1024,256]{1,0:T(8,128)(2,1)S(1)}, bf16[1024,256]{1,0:T(8,128)(2,1)S(1)}, u32[]{:S(2)}, u32[]{:S(2)}) collective-permute-start(bf16[1024,256]{1,0:T(8,128)(2,1)S(1)} %shard_map.53.mine_ref), channel_id=1, source_target_pairs={{0,1},{1,0},{2,3},{3,2},{4,5},{5,4},{6,7},{7,6},{8,9},{9,8},{10,11... | collective-permute-start | bytes 1572872 | tf_op jit(solution)/shard_map/ppermute | solution.py:250

commit v3 on v2

--- a/solution.py
+++ b/solution.py
@@ -98,24 +98,58 @@
     )(info, *blocks)
 
 
-def moment_kernel(tile, info_ref, w_ref, mine_ref, other_ref, x_ref, out_ref, lhs):
-    users, items = x_ref.shape
-    half = users // CORES
-    lanes16 = w_ref[...]
-    wrow = jnp.concatenate([lanes16[k : k + 1, :] for k in range(users // LANES)], axis=1)
-    wrow32 = wrow.astype(F32)
-    count = jnp.sum(wrow32, axis=1, keepdims=True)
-    total = jnp.zeros((P_SIZE, LANES), F32)
-    first = info_ref[CORE] == 0
-    low = jnp.where(first, mine_ref[...], other_ref[...])
-    high = jnp.where(first, other_ref[...], mine_ref[...])
-    for k, part in enumerate((low, high)):
-        cut = slice(k * half, (k + 1) * half)
-        product = part.T.astype(F32) * wrow32[:, cut]
-        lhs[0:P_SIZE, cut] = product.astype(BF16)
-        for g in range(0, half, LANES):
-            total += product[:, g : g + LANES]
-    lhs[P_SIZE:, :] = jnp.broadcast_to(wrow, (16, users))
+def left_side(core, w_ref, block_ref, lhs):
+    half = block_ref.shape[0]
+    lanes16 = w_ref[...].astype(F32)
+    per = half // LANES
+    rows = jnp.where(core == 0, lanes16[0:per], lanes16[per:])
+    wrow = jnp.concatenate([rows[k : k + 1, :] for k in range(per)], axis=1)
+    product = block_ref[...].T.astype(F32) * wrow
+    lhs[0:P_SIZE, :] = product.astype(BF16)
+    lhs[P_SIZE:, :] = jnp.broadcast_to(wrow, (16, half)).astype(BF16)
+    total = product[:, 0:LANES]
+    for g in range(LANES, half, LANES):
+        total += product[:, g : g + LANES]
+    return total
+
+
+def own_kernel(tile, info_ref, w_ref, block_ref, x_ref, acc_ref, total_ref, lhs):
+    half, core = block_ref.shape[0], info_ref[CORE]
+    total_ref[...] = left_side(core, w_ref, block_ref, lhs)
+    users = pl.ds(pl.multiple_of(core * half, half), half)
+    for t in range(x_ref.shape[1] // tile):
+        cut = slice(t * tile, (t + 1) * tile)
+        acc_ref[:, cut] = jnp.dot(lhs[...], x_ref[users, cut], preferred_element_type=F32)
+
+
+def own_half(info, x, block, weights):
+    users, items = x.shape
+    return pl.pallas_call(
+        functools.partial(own_kernel, 512),
+        in_specs=[pl.BlockSpec(memory_space=pltpu.SMEM)]
+        + [pl.BlockSpec(memory_space=pltpu.VMEM)] * 3,
+        out_specs=[pl.BlockSpec(memory_space=pltpu.VMEM)] * 2,
+        out_shape=[
+            jax.ShapeDtypeStruct((P_SIZE + 16, items), F32),
+            jax.ShapeDtypeStruct((P_SIZE, LANES), F32),
+        ],
+        scratch_shapes=[pltpu.VMEM((P_SIZE + 16, users // CORES), BF16)],
+        compiler_params=pltpu.CompilerParams(vmem_limit_bytes=12 * 2**20),
+        cost_estimate=pl.CostEstimate(
+            flops=users * items * P_SIZE, bytes_accessed=4 * 2**20, transcendentals=0
+        ),
+    )(info, weights.reshape(-1, LANES), block, x)
+
+
+def moment_kernel(
+    tile, info_ref, w_ref, block_ref, x_ref, acc_ref, total_ref, out_ref, lhs
+):
+    items = x_ref.shape[1]
+    half, core = block_ref.shape[0], 1 - info_ref[CORE]
+    total = total_ref[...] + left_side(core, w_ref, block_ref, lhs)
+    users = pl.ds(pl.multiple_of(core * half, half), half)
+    weights = w_ref[...].astype(F32)
+    count = jnp.sum(jnp.sum(weights, axis=0, keepdims=True), axis=1, keepdims=True)
     inverse = 1.0 / count
     pcol = jnp.sum(total, axis=1, keepdims=True) * inverse
     prow = jnp.broadcast_to(pcol, (P_SIZE, LANES)).T[0:1, :]
@@ -132,8 +166,9 @@
     pieces = tile // BLK
 
     for t in range(items // tile):
-        acc = jnp.dot(
-            lhs[...], x_ref[:, t * tile : (t + 1) * tile], preferred_element_type=F32
+        cut = slice(t * tile, (t + 1) * tile)
+        acc = acc_ref[:, cut] + jnp.dot(
+            lhs[...], x_ref[users, cut], preferred_element_type=F32
         )
         mrow = acc[P_SIZE : P_SIZE + 1, :] * inverse
         moment = acc[0:P_SIZE, :] * inverse - pcol * mrow
@@ -164,20 +199,21 @@
 
 
 def moments(info, x, mine, other, weights, pieces):
+    acc, total = own_half(info, x, mine, weights)
     users, items = x.shape
     tile = 512
     return pl.pallas_call(
         functools.partial(moment_kernel, tile),
         in_specs=[pl.BlockSpec(memory_space=pltpu.SMEM)]
-        + [pl.BlockSpec(memory_space=pltpu.VMEM)] * 4,
+        + [pl.BlockSpec(memory_space=pltpu.VMEM)] * 5,
         out_specs=pl.BlockSpec(memory_space=pltpu.VMEM),
         out_shape=jax.ShapeDtypeStruct((pieces, 2 * BLK + EXTRA, LANES), BF16),
-        scratch_shapes=[pltpu.VMEM((P_SIZE + 16, users), BF16)],
+        scratch_shapes=[pltpu.VMEM((P_SIZE + 16, users // CORES), BF16)],
         compiler_params=pltpu.CompilerParams(vmem_limit_bytes=16 * 2**20),
         cost_estimate=pl.CostEstimate(
-            flops=2 * users * items * P_SIZE, bytes_accessed=4 * 2**20, transcendentals=0
+            flops=users * items * P_SIZE, bytes_accessed=4 * 2**20, transcendentals=0
         ),
-    )(info, weights.reshape(-1, LANES), mine, other, x)
+    )(info, weights.reshape(-1, LANES), other, x, acc, total)
 
 
 def merge_kernel(groups, cycles, in_ref, cov_ref, mean_ref):
@@ -195,17 +231,21 @@
         mean_all = jnp.sum(share * mean, axis=0, keepdims=True)
         mean_ref[i : i + 1, :] = mean_all
         left = jnp.broadcast_to(share, (groups, 32)) * (mean - mean_all)
-        left = jnp.concatenate([left] * 4, axis=1).T
+        between = lax.dot_general(
+            left,
+            panel_dev,
+            (((0,), (0,)), ((), ())),
+            precision=lax.Precision.HIGHEST,
+            preferred_element_type=F32,
+        )
         back = share / stats[:, 7, 96:97]
-        first = jnp.zeros((BLK, LANES), F32)
-        second = jnp.zeros((BLK, LANES), F32)
+        within = jnp.zeros((2 * BLK, LANES), F32)
         for u in range(groups):
             y = in_ref[u, i, 0 : 2 * BLK, :].astype(F32)
-            size = jnp.exp2(jnp.log2(jnp.abs(y)) * 0.125)
-            v = jnp.where(y < 0, -size, size) * back[u : u + 1, :]
-            col = left[0:BLK, u : u + 1]
-            first = first + v[0:BLK] + col * panel_dev[u : u + 1, 0:LANES]
-            second = second + v[BLK:] + col * panel_dev[u : u + 1, LANES:]
+            shrink = jnp.exp2(-0.875 * jnp.log2(jnp.maximum(jnp.abs(y), 1e-37)))
+            within = within + (y * back[u : u + 1, :]) * shrink
+        first = within[0:BLK] + between[:, 0:LANES]
+        second = within[BLK:] + between[:, LANES:]
         cov_ref[i, :, 0:LANES] = first
         cov_ref[i, :, LANES:] = second
 

time: 89.8 us -> 87.2 us (0.971)
  waiting for transfers between devices: 16.1 us -> 14.5 us
    pallas_call x0 -> x1, Pallas kernels: none -> 3.1 us  [own_half(): pl.pallas_call(functools.partial(own_kernel, 512), in_specs=[pl.BlockSpec...]
    pallas_call x1, Pallas kernels: 7.41 us -> 4.65 us  [moments(): pl.pallas_call(functools.partial(moment_kernel, tile), in_specs=[pl.Block...]
    ppermute x1, waiting for transfers between devices: 1.54 us -> 0.01 us  [spread_panel(): return (mine, lax.ppermute(mine, 'items', across))]
    pallas_call x1, Pallas kernels: 3.49 us -> 2.42 us  [merge(): pl.pallas_call(functools.partial(merge_kernel, groups, cycles), out_shape...]
  transfers between devices with their start and end apart: 6 -> 6, of which waited for: 5 -> 4; matrix products, arithmetic and copies ran while one was open for 0% -> 0% of each run, Pallas kernels for 0% -> 4%
where the time goes in v3:
time: 87.2 us; the launch traced here: 87 us
  blocking collectives  43 us (49%)
  waiting for transfers between devices  14.5 us (17%)
  Pallas kernels  11.4 us (13%)
  starting transfers between devices  9.65 us (11%)
  local copies, waits for them, and re-layouts  7.06 us (8%)
  between operations  1.38 us (2%)
    all_to_all x1, blocking collectives, per_device(): moved = lax.all_to_all(pieces, ('users', 'items'), 0, 0, tiled=True)  43 us
    ppermute x4, waiting for transfers between devices, step(): return lax.ppermute(block, 'items', pairs)  13.1 us
    unnamed x6, local copies, waits for them, and re-layouts  5.78 us
    ppermute x4, starting transfers between devices, step(): return lax.ppermute(block, 'items', pairs)  5.63 us
    pallas_call x1, Pallas kernels, moments(): pl.pallas_call(functools.partial(moment_kernel, tile), in_specs=[pl.Block...  4.65 us
    pallas_call x1, Pallas kernels, own_half(): pl.pallas_call(functools.partial(own_kernel, 512), in_specs=[pl.BlockSpec...  3.1 us
    ppermute x1, starting transfers between devices, spread_panel(): return (mine, lax.ppermute(mine, 'items', across))  2.53 us
    pallas_call x1, Pallas kernels, merge(): pl.pallas_call(functools.partial(merge_kernel, groups, cycles), out_shape...  2.42 us
  transfers between devices with their start and end apart: 6, of which 4 were waited for; matrix products, arithmetic and copies ran while one was open for 0% of the time, Pallas kernels for 4%

profile of v3, /device:TPU:1, one launch (start us, length us, event | category | flops | bytes accessed | tf_op | source)
XLA Modules:
  0.0 87.0 jit_solution(14782078998198732968)
XLA Ops:
  1.3 1.3 %fusion = (bf16[1024,256]{1,0:T(8,128)(2,1)S(1)}, bf16[1024,256]{1,0:T(8,128)(2,1)S(1)}) fusion(bf16[2048,4096]{1,0:T(8,128)(2,1)} %x_ref.5, s32[]{:T(128)S(6)} %select_n.48, s32[]{:T(128)S(6)} %select_n.47, s32[]{:T(128)S(6)} %select_n.45), kind=kLoop, calls=%fused_computation.1 | loop fusion | bytes 2097164 | tf_op jit(solution)/shard_map/dynamic_slice | solution.py:284
  2.6 1.5 %collective-permute-start = (bf16[1024,256]{1,0:T(8,128)(2,1)S(1)}, bf16[1024,256]{1,0:T(8,128)(2,1)S(1)}, u32[]{:S(2)}, u32[]{:S(2)}) collective-permute-start(bf16[1024,256]{1,0:T(8,128)(2,1)S(1)} %get-tuple-element.10), channel_id=1, source_target_pairs={{0,1},{1,0},{2,3},{3,2},{4,5},{5,4},{6,7},{7,6},{8,9},{9,8},{10,11... | collective-permute-start | bytes 1572872 | tf_op jit(solution)/shard_map/ppermute | solution.py:285
  4.1 0.1 pad_add_fusion.info_ref
  4.2 1.5 %collective-permute-done.got_ref = bf16[1024,256]{1,0:T(8,128)(2,1)S(1)} collective-permute-done((bf16[1024,256]{1,0:T(8,128)(2,1)S(1)}, bf16[1024,256]{1,0:T(8,128)(2,1)S(1)}, u32[]{:S(2)}, u32[]{:S(2)}) %collective-permute-start) | collective-permute-done | bytes 524320 | tf_op jit(solution)/shard_map/ppermute | solution.py:285
  5.6 0.0 copy-start.2
  5.6 0.6 shard_map.50.after_ref.mine_ref
  6.2 2.9 %collective-permute-start.2 = (bf16[1024,256]{1,0:T(8,128)(2,1)S(1)}, bf16[1024,256]{1,0:T(8,128)(2,1)S(1)}, u32[]{:S(2)}, u32[]{:S(2)}) collective-permute-start(bf16[1024,256]{1,0:T(8,128)(2,1)S(1)} %shard_map.50.after_ref.mine_ref), channel_id=1, source_target_pairs={{0,6},{1,7},{2,0},{3,1},{4,2},{5,3},{6,4},{7,5},{8,14},{9,15},{10,... | collective-permute-start | bytes 1572872 | tf_op jit(solution)/shard_map/ppermute | solution.py:281
  9.1 0.0 collective-permute-start.1
  9.1 0.0 copy-start
  9.1 5.8 %copy-done = bf16[2048,4096]{1,0:T(8,128)(2,1)S(1)} copy-done((bf16[2048,4096]{1,0:T(8,128)(2,1)S(1)}, bf16[2048,4096]{1,0:T(8,128)(2,1)}, u32[]{:S(2)}) %copy-start) | copy-done | bytes 16777240
  14.9 0.0 copy-start.1
  14.9 5.2 %collective-permute-done.2.left_ref = bf16[1024,256]{1,0:T(8,128)(2,1)S(1)} collective-permute-done((bf16[1024,256]{1,0:T(8,128)(2,1)S(1)}, bf16[1024,256]{1,0:T(8,128)(2,1)S(1)}, u32[]{:S(2)}, u32[]{:S(2)}) %collective-permute-start.2) | collective-permute-done | bytes 524320 | tf_op jit(solution)/shard_map/ppermute | solution.py:281
  20.1 3.1 %collective-permute-done.1.right_ref = bf16[1024,256]{1,0:T(8,128)(2,1)S(1)} collective-permute-done((bf16[1024,256]{1,0:T(8,128)(2,1)S(1)}, bf16[1024,256]{1,0:T(8,128)(2,1)S(1)}, u32[]{:S(2)}, u32[]{:S(2)}) %collective-permute-start.1) | collective-permute-done | bytes 524320 | tf_op jit(solution)/shard_map/ppermute | solution.py:281
  23.2 0.1 collective-permute-start.3
  23.3 2.7 %collective-permute-start.4 = (bf16[512,256]{1,0:T(8,128)(2,1)S(1)}, bf16[512,256]{1,0:T(8,128)(2,1)S(1)}, u32[]{:S(2)}, u32[]{:S(2)}) collective-permute-start(bf16[512,256]{1,0:T(8,128)(2,1)S(1)} %get-tuple-element.7), channel_id=1, source_target_pairs={{0,6},{1,7},{2,0},{3,1},{4,2},{5,3},{6,4},{7,5},{8,14},{9,15},{10,... | collective-permute-start | bytes 786440 | tf_op jit(solution)/shard_map/ppermute | solution.py:281
  25.9 4.8 %collective-permute-done.3.far_a_ref = bf16[512,256]{1,0:T(8,128)(2,1)S(1)} collective-permute-done((bf16[512,256]{1,0:T(8,128)(2,1)S(1)}, bf16[512,256]{1,0:T(8,128)(2,1)S(1)}, u32[]{:S(2)}, u32[]{:S(2)}) %collective-permute-start.3) | collective-permute-done | bytes 262176 | tf_op jit(solution)/shard_map/ppermute | solution.py:281
  30.7 0.0 collective-permute-done.4.far_b_ref
  30.8 0.6 shard_map.53.block_ref
  31.4 2.5 %collective-permute-start.5 = (bf16[1024,256]{1,0:T(8,128)(2,1)S(1)}, bf16[1024,256]{1,0:T(8,128)(2,1)S(1)}, u32[]{:S(2)}, u32[]{:S(2)}) collective-permute-start(bf16[1024,256]{1,0:T(8,128)(2,1)S(1)} %shard_map.53.block_ref), channel_id=1, source_target_pairs={{0,1},{1,0},{2,3},{3,2},{4,5},{5,4},{6,7},{7,6},{8,9},{9,8},{10,11... | collective-permute-start | bytes 1572872 | tf_op jit(solution)/shard_map/ppermute | solution.py:290
  33.9 0.0 copy-done.2
  33.9 0.0 copy-done.1
  33.9 3.1 %shard_map.54 = (f32[272,4096]{1,0:T(8,128)S(1)}, f32[256,128]{1,0:T(8,128)S(1)}) custom-call(s32[3]{0:T(128)S(1)} %pad_add_fusion.info_ref, bf16[16,128]{1,0:T(8,128)(2,1)S(1)} %bitcast.11, bf16[1024,256]{1,0:T(8,128)(2,1)S(1)} %shard_map.53.block_ref, bf16[2048,4096]{1,0:T(8,128)(2,1)S(1)} %copy-done.1), custom_call_target="tpu_custom_call" | custom-call | flops 2147483648 | bytes 4194304 | tf_op jit(solution)/shard_map/pallas_call | solution.py:127
  37.0 0.0 collective-permute-done.5.block_ref
  37.0 4.6 %shard_map.55 = bf16[128,72,128]{2,1,0:T(8,128)(2,1)S(1)} custom-call(s32[3]{0:T(128)S(1)} %pad_add_fusion.info_ref, bf16[16,128]{1,0:T(8,128)(2,1)S(1)} %bitcast.12, bf16[1024,256]{1,0:T(8,128)(2,1)S(1)} %collective-permute-done.5.block_ref, bf16[2048,4096]{1,0:T(8,128)(2,1)S(1)} %copy-done.1, f32[272,4096]{1,0:T(8,128)S(1)} %get-tuple-element.8.acc_ref, ...), custom_call_target="tpu_custom_call" | custom-call | flops 2147483648 | bytes 4194304 | tf_op jit(solution)/shard_map/pallas_call | solution.py:205
  41.7 43.0 %all_to_all.5 = bf16[128,72,128]{2,1,0:T(8,128)(2,1)S(1)} all-to-all(bf16[128,72,128]{2,1,0:T(8,128)(2,1)S(1)} %shard_map.55), channel_id=1, replica_groups=mesh['users'=16,'items'=8] {'users','items'}, dimensions={0} | all-to-all | bytes 4718592 | tf_op jit(solution)/shard_map/all_to_all | solution.py:304
  84.6 2.4 %shard_map.56 = (f32[8,32,256]{2,1,0:T(8,128)}, f32[8,32]{1,0:T(8,128)}) custom-call(bf16[16,8,72,128]{3,2,1,0:T(8,128)(2,1)S(1)} %bitcast.10), custom_call_target="tpu_custom_call" | custom-call | flops 20971520 | bytes 3145728 | tf_op jit(solution)/shard_map/pallas_call | solution.py:254
  (2 shorter events, 0.0 us)
Async XLA Ops:
  2.6 3.0 %collective-permute-start = (bf16[1024,256]{1,0:T(8,128)(2,1)S(1)}, bf16[1024,256]{1,0:T(8,128)(2,1)S(1)}, u32[]{:S(2)}, u32[]{:S(2)}) collective-permute-start(bf16[1024,256]{1,0:T(8,128)(2,1)S(1)} %get-tuple-element.10), channel_id=1, source_target_pairs={{0,1},{1,0},{2,3},{3,2},{4,5},{5,4},{6,7},{7,6},{8,9},{9,8},{10,11... | collective-permute-start | bytes 1572872 | tf_op jit(solution)/shard_map/ppermute | solution.py:285
  5.6 28.2 %copy-start.2 = (bf16[2048]{0:T(1024)(128)(2,1)S(1)}, bf16[2048]{0:T(1024)(128)(2,1)}, u32[]{:S(2)}) copy-start(bf16[2048]{0:T(1024)(128)(2,1)} %param.4) | copy-start | bytes 12292
  6.2 13.8 %collective-permute-start.2 = (bf16[1024,256]{1,0:T(8,128)(2,1)S(1)}, bf16[1024,256]{1,0:T(8,128)(2,1)S(1)}, u32[]{:S(2)}, u32[]{:S(2)}) collective-permute-start(bf16[1024,256]{1,0:T(8,128)(2,1)S(1)} %shard_map.50.after_ref.mine_ref), channel_id=1, source_target_pairs={{0,6},{1,7},{2,0},{3,1},{4,2},{5,3},{6,4},{7,5},{8,14},{9,15},{10,... | collective-permute-start | bytes 1572872 | tf_op jit(solution)/shard_map/ppermute | solution.py:281
  9.1 14.0 %collective-permute-start.1 = (bf16[1024,256]{1,0:T(8,128)(2,1)S(1)}, bf16[1024,256]{1,0:T(8,128)(2,1)S(1)}, u32[]{:S(2)}, u32[]{:S(2)}) collective-permute-start(bf16[1024,256]{1,0:T(8,128)(2,1)S(1)} %shard_map.50.after_ref.mine_ref), channel_id=1, source_target_pairs={{0,2},{1,3},{2,4},{3,5},{4,6},{5,7},{6,0},{7,1},{8,10},{9,11},{10,... | collective-permute-start | bytes 1572872 | tf_op jit(solution)/shard_map/ppermute | solution.py:281
  9.1 5.8 %copy-start = (bf16[2048,4096]{1,0:T(8,128)(2,1)S(1)}, bf16[2048,4096]{1,0:T(8,128)(2,1)}, u32[]{:S(2)}) copy-start(bf16[2048,4096]{1,0:T(8,128)(2,1)} %x_ref.5) | copy-start | bytes 50331652
  14.9 19.0 %copy-start.1 = (bf16[2048,4096]{1,0:T(8,128)(2,1)S(1)}, bf16[2048,4096]{1,0:T(8,128)(2,1)}, u32[]{:S(2)}) copy-start(bf16[2048,4096]{1,0:T(8,128)(2,1)} %x_ref.5) | copy-start | bytes 50331652
  23.2 7.6 %collective-permute-start.3 = (bf16[512,256]{1,0:T(8,128)(2,1)S(1)}, bf16[512,256]{1,0:T(8,128)(2,1)S(1)}, u32[]{:S(2)}, u32[]{:S(2)}) collective-permute-start(bf16[512,256]{1,0:T(8,128)(2,1)S(1)} %get-tuple-element.6), channel_id=1, source_target_pairs={{0,2},{1,3},{2,4},{3,5},{4,6},{5,7},{6,0},{7,1},{8,10},{9,11},{10,... | collective-permute-start | bytes 786440 | tf_op jit(solution)/shard_map/ppermute | solution.py:281
  23.3 7.5 %collective-permute-start.4 = (bf16[512,256]{1,0:T(8,128)(2,1)S(1)}, bf16[512,256]{1,0:T(8,128)(2,1)S(1)}, u32[]{:S(2)}, u32[]{:S(2)}) collective-permute-start(bf16[512,256]{1,0:T(8,128)(2,1)S(1)} %get-tuple-element.7), channel_id=1, source_target_pairs={{0,6},{1,7},{2,0},{3,1},{4,2},{5,3},{6,4},{7,5},{8,14},{9,15},{10,... | collective-permute-start | bytes 786440 | tf_op jit(solution)/shard_map/ppermute | solution.py:281
  31.4 5.6 %collective-permute-start.5 = (bf16[1024,256]{1,0:T(8,128)(2,1)S(1)}, bf16[1024,256]{1,0:T(8,128)(2,1)S(1)}, u32[]{:S(2)}, u32[]{:S(2)}) collective-permute-start(bf16[1024,256]{1,0:T(8,128)(2,1)S(1)} %shard_map.53.block_ref), channel_id=1, source_target_pairs={{0,1},{1,0},{2,3},{3,2},{4,5},{5,4},{6,7},{7,6},{8,9},{9,8},{10,11... | collective-permute-start | bytes 1572872 | tf_op jit(solution)/shard_map/ppermute | solution.py:290

commit v4 on v3

--- a/solution.py
+++ b/solution.py
@@ -5,16 +5,27 @@
 from jax import lax
 from jax.experimental import pallas as pl
 from jax.experimental.pallas import tpu as pltpu
+from jax.sharding import Mesh
 from jax.sharding import PartitionSpec as P
 
 P_SIZE = 256
 BLK = 32
 LANES = 128
 CORES = 2
+USERS, ITEMS = ("z", "x"), ("y", "c")
+ORDER = ("c", "y", "x", "z")
 CORE, AWAY, SAME = range(3)
 EXTRA = 8
 F32 = jnp.float32
 BF16 = jnp.bfloat16
+
+
+def slot(owner):
+    place = dict(zip(USERS + ITEMS, (owner // 32, owner // 8 % 4, owner // 2 % 4, owner % 2)))
+    index = 0
+    for axis in ORDER:
+        index = index * (CORES if axis == "c" else 4) + place[axis]
+    return index
 
 
 def split3(value):
@@ -177,9 +188,10 @@
         v = moment * scale
         v2 = v * v
         coded = (v * jnp.abs(v) * v2 * (v2 * v2)).astype(BF16).T.reshape(pieces, BLK, P_SIZE)
-        place = slice(t * pieces, (t + 1) * pieces)
-        out_ref[place, 0:BLK, :] = coded[:, :, 0:LANES]
-        out_ref[place, BLK : 2 * BLK, :] = coded[:, :, LANES:]
+        for k in range(pieces):
+            place = slot(t * pieces + k)
+            out_ref[place, 0:BLK, :] = coded[k, :, 0:LANES]
+            out_ref[place, BLK : 2 * BLK, :] = coded[k, :, LANES:]
         hi, mid, lo = split3(mrow)
         base = jnp.where((row8 == 7) & (lane8 >= 96), scale, fixed)
         for q in range(per):
@@ -195,7 +207,7 @@
             for g in range(tile // LANES):
                 row = jnp.broadcast_to(mix[:, g * LANES : (g + 1) * LANES], (EXTRA, LANES))
                 stats = jnp.where(row8 == 6, row, base).astype(BF16)
-                out_ref[t * pieces + g * per + q, 2 * BLK :, :] = stats
+                out_ref[slot(t * pieces + g * per + q), 2 * BLK :, :] = stats
 
 
 def moments(info, x, mine, other, weights, pieces):
@@ -217,7 +229,7 @@
 
 
 def merge_kernel(groups, cycles, in_ref, cov_ref, mean_ref):
-    stats0 = in_ref[:, 0, 2 * BLK :, :].astype(F32)
+    stats0 = in_ref[0, :, 2 * BLK :, :].astype(F32)
     part = lambda row: jnp.concatenate([stats0[:, row, :], stats0[:, row + 1, :]], axis=1)
     panel = part(0) + part(2) + part(4)
     last = stats0[:, 7, :]
@@ -225,7 +237,8 @@
     share = count / jnp.sum(count, axis=0, keepdims=True)
     panel_dev = panel - jnp.sum(share * panel, axis=0, keepdims=True)
     for i in range(cycles):
-        stats = in_ref[:, i, 2 * BLK :, :].astype(F32)
+        at = i % CORES * (cycles // CORES) + i // CORES
+        stats = in_ref[at, :, 2 * BLK :, :].astype(F32)
         row = stats[:, 6, :]
         mean = row[:, 0:32] + row[:, 32:64] + row[:, 64:96]
         mean_all = jnp.sum(share * mean, axis=0, keepdims=True)
@@ -241,7 +254,7 @@
         back = share / stats[:, 7, 96:97]
         within = jnp.zeros((2 * BLK, LANES), F32)
         for u in range(groups):
-            y = in_ref[u, i, 0 : 2 * BLK, :].astype(F32)
+            y = in_ref[at, u, 0 : 2 * BLK, :].astype(F32)
             shrink = jnp.exp2(-0.875 * jnp.log2(jnp.maximum(jnp.abs(y), 1e-37)))
             within = within + (y * back[u : u + 1, :]) * shrink
         first = within[0:BLK] + between[:, 0:LANES]
@@ -263,11 +276,11 @@
         cost_estimate=pl.CostEstimate(
             flops=20 * 2**20, bytes_accessed=3 * 2**20, transcendentals=2 * 2**20
         ),
-    )(pieces.reshape(groups, cycles, *pieces.shape[1:]))
+    )(pieces.reshape(cycles, groups, *pieces.shape[1:]))
 
 
 def spread_panel(x, info, core, start):
-    ring = lax.axis_size("items")
+    ring = lax.axis_size(ITEMS)
     chips = ring // CORES
     half = x.shape[0] // CORES
     across = [(i, i ^ 1) for i in range(ring)]
@@ -278,21 +291,21 @@
             for y in range(chips)
             for c in range(CORES)
         ]
-        return lax.ppermute(block, "items", pairs)
+        return lax.ppermute(block, ITEMS, pairs)
 
     own = lax.dynamic_slice(x, (core * half, start), (half, P_SIZE))
     other = lax.dynamic_slice(x, ((1 - core) * half, start), (half, P_SIZE))
-    mine = select(choose_kernel, info, own, lax.ppermute(other, "items", across))
+    mine = select(choose_kernel, info, own, lax.ppermute(other, ITEMS, across))
     right, left = step(mine, 1), step(mine, -1)
     first, second = turn(right, left, touch(x, mine))
     far_a, far_b = step(first, 1), step(second, -1)
     mine = select(join_kernel, info, mine, right, left, far_a, far_b)
-    return mine, lax.ppermute(mine, "items", across)
+    return mine, lax.ppermute(mine, ITEMS, across)
 
 
 def per_device(interactions, user_weights, panel_index):
-    groups, ring = lax.axis_size("users"), lax.axis_size("items")
-    me, chips = lax.axis_index("items"), ring // CORES
+    groups, ring = lax.axis_size(USERS), lax.axis_size(ITEMS)
+    me, chips = lax.axis_index(ITEMS), ring // CORES
     per_shard = interactions.shape[1] // P_SIZE
     owner, place = panel_index[0] // per_shard, panel_index[0] % per_shard
     core = me % CORES
@@ -301,15 +314,16 @@
     info = jnp.stack([core, away, same]).astype(jnp.int32)
     mine, other = spread_panel(interactions, info, core, place * P_SIZE)
     pieces = moments(info, interactions, mine, other, user_weights, groups * ring)
-    moved = lax.all_to_all(pieces, ("users", "items"), 0, 0, tiled=True)
+    moved = lax.all_to_all(pieces, ORDER, 0, 0, tiled=True)
     return tuple(merge(moved, groups, ring))
 
 
 def solution(mesh):
+    split = Mesh(mesh.devices.reshape(4, 4, 4, CORES), USERS + ITEMS)
     return jax.shard_map(
         per_device,
-        mesh=mesh,
-        in_specs=(P("users", "items"), P("users"), P()),
-        out_specs=(P(None, ("users", "items"), None), P(None, ("users", "items"))),
+        mesh=split,
+        in_specs=(P(USERS, ITEMS), P(USERS), P()),
+        out_specs=(P(None, USERS + ITEMS, None), P(None, USERS + ITEMS)),
         check_vma=False,
     )

time: 87.2 us -> 85.5 us (0.981)
  blocking collectives: 43 us -> 41.2 us
    all_to_all x1, blocking collectives: 43 us -> 41.2 us  [per_device(): moved = lax.all_to_all(pieces, ORDER, 0, 0, tiled=True)]
where the time goes in v4:
time: 85.5 us; the launch traced here: 85.3 us
  blocking collectives  41.2 us (48%)
  waiting for transfers between devices  14.5 us (17%)
  Pallas kernels  11.4 us (13%)
  starting transfers between devices  9.65 us (11%)
  local copies, waits for them, and re-layouts  7.06 us (8%)
  between operations  1.38 us (2%)
    all_to_all x1, blocking collectives, per_device(): moved = lax.all_to_all(pieces, ORDER, 0, 0, tiled=True)  41.2 us
    ppermute x4, waiting for transfers between devices, step(): return lax.ppermute(block, ITEMS, pairs)  13.1 us
    unnamed x6, local copies, waits for them, and re-layouts  5.78 us
    ppermute x4, starting transfers between devices, step(): return lax.ppermute(block, ITEMS, pairs)  5.63 us
    pallas_call x1, Pallas kernels, moments(): pl.pallas_call(functools.partial(moment_kernel, tile), in_specs=[pl.Block...  4.65 us
    pallas_call x1, Pallas kernels, own_half(): pl.pallas_call(functools.partial(own_kernel, 512), in_specs=[pl.BlockSpec...  3.1 us
    ppermute x1, starting transfers between devices, spread_panel(): return (mine, lax.ppermute(mine, ITEMS, across))  2.53 us
    pallas_call x1, Pallas kernels, merge(): pl.pallas_call(functools.partial(merge_kernel, groups, cycles), out_shape...  2.42 us
  transfers between devices with their start and end apart: 6, of which 4 were waited for; matrix products, arithmetic and copies ran while one was open for 0% of the time, Pallas kernels for 4%

profile of v4, /device:TPU:1, one launch (start us, length us, event | category | flops | bytes accessed | tf_op | source)
XLA Modules:
  0.0 85.3 jit_solution(6041157414216871498)
XLA Ops:
  1.3 1.3 %fusion = (bf16[1024,256]{1,0:T(8,128)(2,1)S(1)}, bf16[1024,256]{1,0:T(8,128)(2,1)S(1)}) fusion(bf16[2048,4096]{1,0:T(8,128)(2,1)} %x_ref.5, s32[]{:T(128)S(6)} %select_n.48, s32[]{:T(128)S(6)} %select_n.47, s32[]{:T(128)S(6)} %select_n.45), kind=kLoop, calls=%fused_computation.1 | loop fusion | bytes 2097164 | tf_op jit(solution)/shard_map/dynamic_slice | solution.py:297
  2.6 1.5 %collective-permute-start = (bf16[1024,256]{1,0:T(8,128)(2,1)S(1)}, bf16[1024,256]{1,0:T(8,128)(2,1)S(1)}, u32[]{:S(2)}, u32[]{:S(2)}) collective-permute-start(bf16[1024,256]{1,0:T(8,128)(2,1)S(1)} %get-tuple-element.10), channel_id=1, source_target_pairs={{0,1},{1,0},{2,3},{3,2},{4,5},{5,4},{6,7},{7,6},{8,9},{9,8},{10,11... | collective-permute-start | bytes 1572872 | tf_op jit(solution)/shard_map/ppermute | solution.py:298
  4.1 0.1 pad_add_fusion.info_ref
  4.2 1.5 %collective-permute-done.got_ref = bf16[1024,256]{1,0:T(8,128)(2,1)S(1)} collective-permute-done((bf16[1024,256]{1,0:T(8,128)(2,1)S(1)}, bf16[1024,256]{1,0:T(8,128)(2,1)S(1)}, u32[]{:S(2)}, u32[]{:S(2)}) %collective-permute-start) | collective-permute-done | bytes 524320 | tf_op jit(solution)/shard_map/ppermute | solution.py:298
  5.7 0.0 copy-start.2
  5.7 0.6 shard_map.50.after_ref.mine_ref
  6.2 2.9 %collective-permute-start.2 = (bf16[1024,256]{1,0:T(8,128)(2,1)S(1)}, bf16[1024,256]{1,0:T(8,128)(2,1)S(1)}, u32[]{:S(2)}, u32[]{:S(2)}) collective-permute-start(bf16[1024,256]{1,0:T(8,128)(2,1)S(1)} %shard_map.50.after_ref.mine_ref), channel_id=1, source_target_pairs={{0,6},{1,7},{2,0},{3,1},{4,2},{5,3},{6,4},{7,5},{8,14},{9,15},{10,... | collective-permute-start | bytes 1572872 | tf_op jit(solution)/shard_map/ppermute | solution.py:294
  9.1 0.0 collective-permute-start.1
  9.1 0.0 copy-start
  9.1 5.8 %copy-done = bf16[2048,4096]{1,0:T(8,128)(2,1)S(1)} copy-done((bf16[2048,4096]{1,0:T(8,128)(2,1)S(1)}, bf16[2048,4096]{1,0:T(8,128)(2,1)}, u32[]{:S(2)}) %copy-start) | copy-done | bytes 16777240
  14.9 0.0 copy-start.1
  14.9 5.2 %collective-permute-done.2.left_ref = bf16[1024,256]{1,0:T(8,128)(2,1)S(1)} collective-permute-done((bf16[1024,256]{1,0:T(8,128)(2,1)S(1)}, bf16[1024,256]{1,0:T(8,128)(2,1)S(1)}, u32[]{:S(2)}, u32[]{:S(2)}) %collective-permute-start.2) | collective-permute-done | bytes 524320 | tf_op jit(solution)/shard_map/ppermute | solution.py:294
  20.1 3.1 %collective-permute-done.1.right_ref = bf16[1024,256]{1,0:T(8,128)(2,1)S(1)} collective-permute-done((bf16[1024,256]{1,0:T(8,128)(2,1)S(1)}, bf16[1024,256]{1,0:T(8,128)(2,1)S(1)}, u32[]{:S(2)}, u32[]{:S(2)}) %collective-permute-start.1) | collective-permute-done | bytes 524320 | tf_op jit(solution)/shard_map/ppermute | solution.py:294
  23.2 0.1 collective-permute-start.3
  23.3 2.7 %collective-permute-start.4 = (bf16[512,256]{1,0:T(8,128)(2,1)S(1)}, bf16[512,256]{1,0:T(8,128)(2,1)S(1)}, u32[]{:S(2)}, u32[]{:S(2)}) collective-permute-start(bf16[512,256]{1,0:T(8,128)(2,1)S(1)} %get-tuple-element.7), channel_id=1, source_target_pairs={{0,6},{1,7},{2,0},{3,1},{4,2},{5,3},{6,4},{7,5},{8,14},{9,15},{10,... | collective-permute-start | bytes 786440 | tf_op jit(solution)/shard_map/ppermute | solution.py:294
  25.9 4.8 %collective-permute-done.3.far_a_ref = bf16[512,256]{1,0:T(8,128)(2,1)S(1)} collective-permute-done((bf16[512,256]{1,0:T(8,128)(2,1)S(1)}, bf16[512,256]{1,0:T(8,128)(2,1)S(1)}, u32[]{:S(2)}, u32[]{:S(2)}) %collective-permute-start.3) | collective-permute-done | bytes 262176 | tf_op jit(solution)/shard_map/ppermute | solution.py:294
  30.8 0.0 collective-permute-done.4.far_b_ref
  30.8 0.6 shard_map.53.block_ref
  31.4 2.5 %collective-permute-start.5 = (bf16[1024,256]{1,0:T(8,128)(2,1)S(1)}, bf16[1024,256]{1,0:T(8,128)(2,1)S(1)}, u32[]{:S(2)}, u32[]{:S(2)}) collective-permute-start(bf16[1024,256]{1,0:T(8,128)(2,1)S(1)} %shard_map.53.block_ref), channel_id=1, source_target_pairs={{0,1},{1,0},{2,3},{3,2},{4,5},{5,4},{6,7},{7,6},{8,9},{9,8},{10,11... | collective-permute-start | bytes 1572872 | tf_op jit(solution)/shard_map/ppermute | solution.py:303
  33.9 0.0 copy-done.2
  33.9 0.0 copy-done.1
  33.9 3.1 %shard_map.54 = (f32[272,4096]{1,0:T(8,128)S(1)}, f32[256,128]{1,0:T(8,128)S(1)}) custom-call(s32[3]{0:T(128)S(1)} %pad_add_fusion.info_ref, bf16[16,128]{1,0:T(8,128)(2,1)S(1)} %bitcast.11, bf16[1024,256]{1,0:T(8,128)(2,1)S(1)} %shard_map.53.block_ref, bf16[2048,4096]{1,0:T(8,128)(2,1)S(1)} %copy-done.1), custom_call_target="tpu_custom_call" | custom-call | flops 2147483648 | bytes 4194304 | tf_op jit(solution)/shard_map/pallas_call | solution.py:138
  37.0 0.0 collective-permute-done.5.block_ref
  37.0 4.6 %shard_map.55 = bf16[128,72,128]{2,1,0:T(8,128)(2,1)S(1)} custom-call(s32[3]{0:T(128)S(1)} %pad_add_fusion.info_ref, bf16[16,128]{1,0:T(8,128)(2,1)S(1)} %bitcast.12, bf16[1024,256]{1,0:T(8,128)(2,1)S(1)} %collective-permute-done.5.block_ref, bf16[2048,4096]{1,0:T(8,128)(2,1)S(1)} %copy-done.1, f32[272,4096]{1,0:T(8,128)S(1)} %get-tuple-element.8.acc_ref, ...), custom_call_target="tpu_custom_call" | custom-call | flops 2147483648 | bytes 4194304 | tf_op jit(solution)/shard_map/pallas_call | solution.py:217
  41.7 41.2 %all_to_all.5 = bf16[128,72,128]{2,1,0:T(8,128)(2,1)S(1)} all-to-all(bf16[128,72,128]{2,1,0:T(8,128)(2,1)S(1)} %shard_map.55), channel_id=1, replica_groups=mesh['z'=4,'x'=4,'y'=4,'c'=2] {'c','y','x','z'}, dimensions={0} | all-to-all | bytes 4718592 | tf_op jit(solution)/shard_map/all_to_all | solution.py:317
  82.8 2.4 %shard_map.56 = (f32[8,32,256]{2,1,0:T(8,128)}, f32[8,32]{1,0:T(8,128)}) custom-call(bf16[8,16,72,128]{3,2,1,0:T(8,128)(2,1)S(1)} %bitcast.10), custom_call_target="tpu_custom_call" | custom-call | flops 20971520 | bytes 3145728 | tf_op jit(solution)/shard_map/pallas_call | solution.py:267
  (2 shorter events, 0.0 us)
Async XLA Ops:
  2.6 3.0 %collective-permute-start = (bf16[1024,256]{1,0:T(8,128)(2,1)S(1)}, bf16[1024,256]{1,0:T(8,128)(2,1)S(1)}, u32[]{:S(2)}, u32[]{:S(2)}) collective-permute-start(bf16[1024,256]{1,0:T(8,128)(2,1)S(1)} %get-tuple-element.10), channel_id=1, source_target_pairs={{0,1},{1,0},{2,3},{3,2},{4,5},{5,4},{6,7},{7,6},{8,9},{9,8},{10,11... | collective-permute-start | bytes 1572872 | tf_op jit(solution)/shard_map/ppermute | solution.py:298
  5.7 28.2 %copy-start.2 = (bf16[2048]{0:T(1024)(128)(2,1)S(1)}, bf16[2048]{0:T(1024)(128)(2,1)}, u32[]{:S(2)}) copy-start(bf16[2048]{0:T(1024)(128)(2,1)} %param.4) | copy-start | bytes 12292
  6.2 13.8 %collective-permute-start.2 = (bf16[1024,256]{1,0:T(8,128)(2,1)S(1)}, bf16[1024,256]{1,0:T(8,128)(2,1)S(1)}, u32[]{:S(2)}, u32[]{:S(2)}) collective-permute-start(bf16[1024,256]{1,0:T(8,128)(2,1)S(1)} %shard_map.50.after_ref.mine_ref), channel_id=1, source_target_pairs={{0,6},{1,7},{2,0},{3,1},{4,2},{5,3},{6,4},{7,5},{8,14},{9,15},{10,... | collective-permute-start | bytes 1572872 | tf_op jit(solution)/shard_map/ppermute | solution.py:294
  9.1 14.0 %collective-permute-start.1 = (bf16[1024,256]{1,0:T(8,128)(2,1)S(1)}, bf16[1024,256]{1,0:T(8,128)(2,1)S(1)}, u32[]{:S(2)}, u32[]{:S(2)}) collective-permute-start(bf16[1024,256]{1,0:T(8,128)(2,1)S(1)} %shard_map.50.after_ref.mine_ref), channel_id=1, source_target_pairs={{0,2},{1,3},{2,4},{3,5},{4,6},{5,7},{6,0},{7,1},{8,10},{9,11},{10,... | collective-permute-start | bytes 1572872 | tf_op jit(solution)/shard_map/ppermute | solution.py:294
  9.1 5.8 %copy-start = (bf16[2048,4096]{1,0:T(8,128)(2,1)S(1)}, bf16[2048,4096]{1,0:T(8,128)(2,1)}, u32[]{:S(2)}) copy-start(bf16[2048,4096]{1,0:T(8,128)(2,1)} %x_ref.5) | copy-start | bytes 50331652
  14.9 19.0 %copy-start.1 = (bf16[2048,4096]{1,0:T(8,128)(2,1)S(1)}, bf16[2048,4096]{1,0:T(8,128)(2,1)}, u32[]{:S(2)}) copy-start(bf16[2048,4096]{1,0:T(8,128)(2,1)} %x_ref.5) | copy-start | bytes 50331652
  23.2 7.6 %collective-permute-start.3 = (bf16[512,256]{1,0:T(8,128)(2,1)S(1)}, bf16[512,256]{1,0:T(8,128)(2,1)S(1)}, u32[]{:S(2)}, u32[]{:S(2)}) collective-permute-start(bf16[512,256]{1,0:T(8,128)(2,1)S(1)} %get-tuple-element.6), channel_id=1, source_target_pairs={{0,2},{1,3},{2,4},{3,5},{4,6},{5,7},{6,0},{7,1},{8,10},{9,11},{10,... | collective-permute-start | bytes 786440 | tf_op jit(solution)/shard_map/ppermute | solution.py:294
  23.3 7.5 %collective-permute-start.4 = (bf16[512,256]{1,0:T(8,128)(2,1)S(1)}, bf16[512,256]{1,0:T(8,128)(2,1)S(1)}, u32[]{:S(2)}, u32[]{:S(2)}) collective-permute-start(bf16[512,256]{1,0:T(8,128)(2,1)S(1)} %get-tuple-element.7), channel_id=1, source_target_pairs={{0,6},{1,7},{2,0},{3,1},{4,2},{5,3},{6,4},{7,5},{8,14},{9,15},{10,... | collective-permute-start | bytes 786440 | tf_op jit(solution)/shard_map/ppermute | solution.py:294
  31.4 5.6 %collective-permute-start.5 = (bf16[1024,256]{1,0:T(8,128)(2,1)S(1)}, bf16[1024,256]{1,0:T(8,128)(2,1)S(1)}, u32[]{:S(2)}, u32[]{:S(2)}) collective-permute-start(bf16[1024,256]{1,0:T(8,128)(2,1)S(1)} %shard_map.53.block_ref), channel_id=1, source_target_pairs={{0,1},{1,0},{2,3},{3,2},{4,5},{5,4},{6,7},{7,6},{8,9},{9,8},{10,11... | collective-permute-start | bytes 1572872 | tf_op jit(solution)/shard_map/ppermute | solution.py:303

commit v5 on v4

--- a/solution.py
+++ b/solution.py
@@ -14,7 +14,7 @@
 CORES = 2
 USERS, ITEMS = ("z", "x"), ("y", "c")
 ORDER = ("c", "y", "x", "z")
-CORE, AWAY, SAME = range(3)
+CORE, AWAY = range(2)
 EXTRA = 8
 F32 = jnp.float32
 BF16 = jnp.bfloat16
@@ -37,21 +37,21 @@
     return parts
 
 
-def touch_kernel(x_ref, after_ref, out_ref):
+def touch_kernel(x_ref, after_ref, info_ref, out_ref):
     out_ref[...] = jnp.zeros_like(out_ref)
 
 
-def touch(x, after):
+def touch(x, *after):
     return pl.pallas_call(
         touch_kernel,
-        in_specs=[pl.BlockSpec(memory_space=pltpu.VMEM), pl.BlockSpec(memory_space=pl.ANY)],
+        in_specs=[pl.BlockSpec(memory_space=pltpu.VMEM)] + [pl.BlockSpec(memory_space=pl.ANY)] * 2,
         out_specs=pl.BlockSpec(memory_space=pltpu.VMEM),
         out_shape=jax.ShapeDtypeStruct((8, LANES), F32),
         compiler_params=pltpu.CompilerParams(vmem_limit_bytes=2 * 2**20),
         cost_estimate=pl.CostEstimate(
             flops=0, bytes_accessed=x.size * x.dtype.itemsize, transcendentals=0
         ),
-    )(x, after)
+    )(x, *after)
 
 
 def turn_kernel(right_ref, left_ref, after_ref, first_ref, second_ref):
@@ -73,16 +73,6 @@
     )(right, left, after)
 
 
-def choose_kernel(info_ref, own_ref, got_ref, out_ref):
-    @pl.when(info_ref[SAME] == 1)
-    def _():
-        out_ref[...] = own_ref[...]
-
-    @pl.when(info_ref[SAME] != 1)
-    def _():
-        out_ref[...] = got_ref[...]
-
-
 def join_kernel(info_ref, mine_ref, right_ref, left_ref, far_a_ref, far_b_ref, out_ref):
     part = far_a_ref.shape[0]
     for k, ref in ((0, mine_ref), (1, right_ref), (3, left_ref)):
@@ -97,9 +87,9 @@
         out_ref[part:, :] = far_b_ref[...]
 
 
-def select(kernel, info, *blocks):
-    return pl.pallas_call(
-        kernel,
+def join(info, *blocks):
+    return pl.pallas_call(
+        join_kernel,
         in_specs=[pl.BlockSpec(memory_space=pltpu.SMEM)]
         + [pl.BlockSpec(memory_space=pltpu.VMEM)] * len(blocks),
         out_specs=pl.BlockSpec(memory_space=pltpu.VMEM),
@@ -176,11 +166,17 @@
     per = LANES // BLK
     pieces = tile // BLK
 
-    for t in range(items // tile):
+    def whole(t):
         cut = slice(t * tile, (t + 1) * tile)
-        acc = acc_ref[:, cut] + jnp.dot(
+        return acc_ref[:, cut] + jnp.dot(
             lhs[...], x_ref[users, cut], preferred_element_type=F32
         )
+
+    later = whole(0)
+    for t in range(items // tile):
+        acc = later
+        if t + 1 < items // tile:
+            later = whole(t + 1)
         mrow = acc[P_SIZE : P_SIZE + 1, :] * inverse
         moment = acc[0:P_SIZE, :] * inverse - pcol * mrow
         top = jnp.max(jnp.max(jnp.abs(moment), axis=0, keepdims=True), axis=1, keepdims=True)
@@ -279,7 +275,7 @@
     )(pieces.reshape(cycles, groups, *pieces.shape[1:]))
 
 
-def spread_panel(x, info, core, start):
+def spread_panel(x, info, core, same, start):
     ring = lax.axis_size(ITEMS)
     chips = ring // CORES
     half = x.shape[0] // CORES
@@ -295,11 +291,12 @@
 
     own = lax.dynamic_slice(x, (core * half, start), (half, P_SIZE))
     other = lax.dynamic_slice(x, ((1 - core) * half, start), (half, P_SIZE))
-    mine = select(choose_kernel, info, own, lax.ppermute(other, ITEMS, across))
+    own, other = lax.optimization_barrier((own, other))
+    mine = jnp.where(same, own, lax.ppermute(other, ITEMS, across))
     right, left = step(mine, 1), step(mine, -1)
-    first, second = turn(right, left, touch(x, mine))
+    first, second = turn(right, left, touch(x, mine, info))
     far_a, far_b = step(first, 1), step(second, -1)
-    mine = select(join_kernel, info, mine, right, left, far_a, far_b)
+    mine = join(info, mine, right, left, far_a, far_b)
     return mine, lax.ppermute(mine, ITEMS, across)
 
 
@@ -310,9 +307,9 @@
     owner, place = panel_index[0] // per_shard, panel_index[0] % per_shard
     core = me % CORES
     away = (me // CORES - owner // CORES) % chips
-    same = (core == owner % CORES).astype(jnp.int32)
-    info = jnp.stack([core, away, same]).astype(jnp.int32)
-    mine, other = spread_panel(interactions, info, core, place * P_SIZE)
+    same = core == owner % CORES
+    info = jnp.stack([core, away]).astype(jnp.int32)
+    mine, other = spread_panel(interactions, info, core, same, place * P_SIZE)
     pieces = moments(info, interactions, mine, other, user_weights, groups * ring)
     moved = lax.all_to_all(pieces, ORDER, 0, 0, tiled=True)
     return tuple(merge(moved, groups, ring))

time: 85.5 us -> 84.9 us (level)
  no operation moved by 1% of the time
where the time goes in v5:
time: 84.9 us; the launch traced here: 84.7 us
  blocking collectives  41.2 us (49%)
  waiting for transfers between devices  14.5 us (17%)
  Pallas kernels  10.8 us (13%)
  starting transfers between devices  9.65 us (11%)
  local copies, waits for them, and re-layouts  7.06 us (8%)
  between operations  1.38 us (2%)
    all_to_all x1, blocking collectives, per_device(): moved = lax.all_to_all(pieces, ORDER, 0, 0, tiled=True)  41.2 us
    ppermute x4, waiting for transfers between devices, step(): return lax.ppermute(block, ITEMS, pairs)  13 us
    unnamed x6, local copies, waits for them, and re-layouts  5.78 us
    ppermute x4, starting transfers between devices, step(): return lax.ppermute(block, ITEMS, pairs)  5.63 us
    pallas_call x1, Pallas kernels, moments(): pl.pallas_call(functools.partial(moment_kernel, tile), in_specs=[pl.Block...  4.62 us
    pallas_call x1, Pallas kernels, own_half(): pl.pallas_call(functools.partial(own_kernel, 512), in_specs=[pl.BlockSpec...  3.09 us
    ppermute x1, starting transfers between devices, spread_panel(): return (mine, lax.ppermute(mine, ITEMS, across))  2.53 us
    pallas_call x1, Pallas kernels, merge(): pl.pallas_call(functools.partial(merge_kernel, groups, cycles), out_shape...  2.42 us
  transfers between devices with their start and end apart: 6, of which 4 were waited for; matrix products, arithmetic and copies ran while one was open for 0% of the time, Pallas kernels for 4%

profile of v5, /device:TPU:1, one launch (start us, length us, event | category | flops | bytes accessed | tf_op | source)
XLA Modules:
  0.0 84.7 jit_solution(17803411053940531734)
XLA Ops:
  1.3 1.3 %fusion = (bf16[1024,256]{1,0:T(8,128)(2,1)S(1)}, bf16[1024,256]{1,0:T(8,128)(2,1)S(1)}) fusion(bf16[2048,4096]{1,0:T(8,128)(2,1)} %x_ref.5, s32[]{:T(128)S(6)} %select_n.57, s32[]{:T(128)S(6)} %select_n.56, s32[]{:T(128)S(6)} %select_n.54), kind=kLoop, calls=%fused_computation.2 | loop fusion | bytes 2097164 | tf_op jit(solution)/shard_map/dynamic_slice | solution.py:293
  2.6 1.5 %collective-permute-start = (bf16[1024,256]{1,0:T(8,128)(2,1)S(1)}, bf16[1024,256]{1,0:T(8,128)(2,1)S(1)}, u32[]{:S(2)}, u32[]{:S(2)}) collective-permute-start(bf16[1024,256]{1,0:T(8,128)(2,1)S(1)} %get-tuple-element.9), channel_id=1, source_target_pairs={{0,1},{1,0},{2,3},{3,2},{4,5},{5,4},{6,7},{7,6},{8,9},{9,8},{10,11... | collective-permute-start | bytes 1572872 | tf_op jit(solution)/shard_map/ppermute | solution.py:295
  4.1 1.5 %collective-permute-done = bf16[1024,256]{1,0:T(8,128)(2,1)S(1)} collective-permute-done((bf16[1024,256]{1,0:T(8,128)(2,1)S(1)}, bf16[1024,256]{1,0:T(8,128)(2,1)S(1)}, u32[]{:S(2)}, u32[]{:S(2)}) %collective-permute-start) | collective-permute-done | bytes 524320 | tf_op jit(solution)/shard_map/ppermute | solution.py:295
  5.7 0.1 broadcast_select_fusion.after_ref.mine_ref
  5.7 2.9 %collective-permute-start.2 = (bf16[1024,256]{1,0:T(8,128)(2,1)S(1)}, bf16[1024,256]{1,0:T(8,128)(2,1)S(1)}, u32[]{:S(2)}, u32[]{:S(2)}) collective-permute-start(bf16[1024,256]{1,0:T(8,128)(2,1)S(1)} %broadcast_select_fusion.after_ref.mine_ref), channel_id=1, source_target_pairs={{0,6},{1,7},{2,0},{3,1},{4,2},{5,3},{6,4},{7,5},{8,14},{9,15},{10,... | collective-permute-start | bytes 1572872 | tf_op jit(solution)/shard_map/ppermute | solution.py:290
  8.6 0.0 collective-permute-start.1
  8.6 0.1 pad_add_fusion.info_ref
  8.7 0.0 copy-start
  8.7 5.8 %copy-done = bf16[2048,4096]{1,0:T(8,128)(2,1)S(1)} copy-done((bf16[2048,4096]{1,0:T(8,128)(2,1)S(1)}, bf16[2048,4096]{1,0:T(8,128)(2,1)}, u32[]{:S(2)}) %copy-start) | copy-done | bytes 16777240
  14.4 0.0 copy-start.1
  14.4 0.0 copy-start.2
  14.5 5.1 %collective-permute-done.2.left_ref = bf16[1024,256]{1,0:T(8,128)(2,1)S(1)} collective-permute-done((bf16[1024,256]{1,0:T(8,128)(2,1)S(1)}, bf16[1024,256]{1,0:T(8,128)(2,1)S(1)}, u32[]{:S(2)}, u32[]{:S(2)}) %collective-permute-start.2) | collective-permute-done | bytes 524320 | tf_op jit(solution)/shard_map/ppermute | solution.py:290
  19.5 3.1 %collective-permute-done.1.right_ref = bf16[1024,256]{1,0:T(8,128)(2,1)S(1)} collective-permute-done((bf16[1024,256]{1,0:T(8,128)(2,1)S(1)}, bf16[1024,256]{1,0:T(8,128)(2,1)S(1)}, u32[]{:S(2)}, u32[]{:S(2)}) %collective-permute-start.1) | collective-permute-done | bytes 524320 | tf_op jit(solution)/shard_map/ppermute | solution.py:290
  22.7 0.1 collective-permute-start.3
  22.7 2.7 %collective-permute-start.4 = (bf16[512,256]{1,0:T(8,128)(2,1)S(1)}, bf16[512,256]{1,0:T(8,128)(2,1)S(1)}, u32[]{:S(2)}, u32[]{:S(2)}) collective-permute-start(bf16[512,256]{1,0:T(8,128)(2,1)S(1)} %get-tuple-element.11), channel_id=1, source_target_pairs={{0,6},{1,7},{2,0},{3,1},{4,2},{5,3},{6,4},{7,5},{8,14},{9,15},{10,... | collective-permute-start | bytes 786440 | tf_op jit(solution)/shard_map/ppermute | solution.py:290
  25.4 4.8 %collective-permute-done.3.far_a_ref = bf16[512,256]{1,0:T(8,128)(2,1)S(1)} collective-permute-done((bf16[512,256]{1,0:T(8,128)(2,1)S(1)}, bf16[512,256]{1,0:T(8,128)(2,1)S(1)}, u32[]{:S(2)}, u32[]{:S(2)}) %collective-permute-start.3) | collective-permute-done | bytes 262176 | tf_op jit(solution)/shard_map/ppermute | solution.py:290
  30.2 0.0 collective-permute-done.4.far_b_ref
  30.2 0.6 shard_map.52.block_ref
  30.8 2.5 %collective-permute-start.5 = (bf16[1024,256]{1,0:T(8,128)(2,1)S(1)}, bf16[1024,256]{1,0:T(8,128)(2,1)S(1)}, u32[]{:S(2)}, u32[]{:S(2)}) collective-permute-start(bf16[1024,256]{1,0:T(8,128)(2,1)S(1)} %shard_map.52.block_ref), channel_id=1, source_target_pairs={{0,1},{1,0},{2,3},{3,2},{4,5},{5,4},{6,7},{7,6},{8,9},{9,8},{10,11... | collective-permute-start | bytes 1572872 | tf_op jit(solution)/shard_map/ppermute | solution.py:300
  33.4 0.0 copy-done.1
  33.4 0.0 copy-done.2
  33.4 3.1 %shard_map.53 = (f32[272,4096]{1,0:T(8,128)S(1)}, f32[256,128]{1,0:T(8,128)S(1)}) custom-call(s32[2]{0:T(128)S(1)} %pad_add_fusion.info_ref, bf16[16,128]{1,0:T(8,128)(2,1)S(1)} %bitcast.10, bf16[1024,256]{1,0:T(8,128)(2,1)S(1)} %shard_map.52.block_ref, bf16[2048,4096]{1,0:T(8,128)(2,1)S(1)} %copy-done.1), custom_call_target="tpu_custom_call" | custom-call | flops 2147483648 | bytes 4194304 | tf_op jit(solution)/shard_map/pallas_call | solution.py:128
  36.5 0.0 collective-permute-done.5.block_ref
  36.5 4.6 %shard_map.54 = bf16[128,72,128]{2,1,0:T(8,128)(2,1)S(1)} custom-call(s32[2]{0:T(128)S(1)} %pad_add_fusion.info_ref, bf16[16,128]{1,0:T(8,128)(2,1)S(1)} %bitcast.11, bf16[1024,256]{1,0:T(8,128)(2,1)S(1)} %collective-permute-done.5.block_ref, bf16[2048,4096]{1,0:T(8,128)(2,1)S(1)} %copy-done.1, f32[272,4096]{1,0:T(8,128)S(1)} %get-tuple-element.12.acc_ref, ...), custom_call_target="tpu_custom_call" | custom-call | flops 2147483648 | bytes 4194304 | tf_op jit(solution)/shard_map/pallas_call | solution.py:213
  41.1 41.2 %all_to_all.5 = bf16[128,72,128]{2,1,0:T(8,128)(2,1)S(1)} all-to-all(bf16[128,72,128]{2,1,0:T(8,128)(2,1)S(1)} %shard_map.54), channel_id=1, replica_groups=mesh['z'=4,'x'=4,'y'=4,'c'=2] {'c','y','x','z'}, dimensions={0} | all-to-all | bytes 4718592 | tf_op jit(solution)/shard_map/all_to_all | solution.py:314
  82.3 2.4 %shard_map.55 = (f32[8,32,256]{2,1,0:T(8,128)}, f32[8,32]{1,0:T(8,128)}) custom-call(bf16[8,16,72,128]{3,2,1,0:T(8,128)(2,1)S(1)} %bitcast.9), custom_call_target="tpu_custom_call" | custom-call | flops 20971520 | bytes 3145728 | tf_op jit(solution)/shard_map/pallas_call | solution.py:263
  (2 shorter events, 0.0 us)
Async XLA Ops:
  2.6 3.0 %collective-permute-start = (bf16[1024,256]{1,0:T(8,128)(2,1)S(1)}, bf16[1024,256]{1,0:T(8,128)(2,1)S(1)}, u32[]{:S(2)}, u32[]{:S(2)}) collective-permute-start(bf16[1024,256]{1,0:T(8,128)(2,1)S(1)} %get-tuple-element.9), channel_id=1, source_target_pairs={{0,1},{1,0},{2,3},{3,2},{4,5},{5,4},{6,7},{7,6},{8,9},{9,8},{10,11... | collective-permute-start | bytes 1572872 | tf_op jit(solution)/shard_map/ppermute | solution.py:295
  5.7 13.8 %collective-permute-start.2 = (bf16[1024,256]{1,0:T(8,128)(2,1)S(1)}, bf16[1024,256]{1,0:T(8,128)(2,1)S(1)}, u32[]{:S(2)}, u32[]{:S(2)}) collective-permute-start(bf16[1024,256]{1,0:T(8,128)(2,1)S(1)} %broadcast_select_fusion.after_ref.mine_ref), channel_id=1, source_target_pairs={{0,6},{1,7},{2,0},{3,1},{4,2},{5,3},{6,4},{7,5},{8,14},{9,15},{10,... | collective-permute-start | bytes 1572872 | tf_op jit(solution)/shard_map/ppermute | solution.py:290
  8.6 14.0 %collective-permute-start.1 = (bf16[1024,256]{1,0:T(8,128)(2,1)S(1)}, bf16[1024,256]{1,0:T(8,128)(2,1)S(1)}, u32[]{:S(2)}, u32[]{:S(2)}) collective-permute-start(bf16[1024,256]{1,0:T(8,128)(2,1)S(1)} %broadcast_select_fusion.after_ref.mine_ref), channel_id=1, source_target_pairs={{0,2},{1,3},{2,4},{3,5},{4,6},{5,7},{6,0},{7,1},{8,10},{9,11},{10,... | collective-permute-start | bytes 1572872 | tf_op jit(solution)/shard_map/ppermute | solution.py:290
  8.7 5.8 %copy-start = (bf16[2048,4096]{1,0:T(8,128)(2,1)S(1)}, bf16[2048,4096]{1,0:T(8,128)(2,1)}, u32[]{:S(2)}) copy-start(bf16[2048,4096]{1,0:T(8,128)(2,1)} %x_ref.5) | copy-start | bytes 50331652
  14.4 18.9 %copy-start.1 = (bf16[2048,4096]{1,0:T(8,128)(2,1)S(1)}, bf16[2048,4096]{1,0:T(8,128)(2,1)}, u32[]{:S(2)}) copy-start(bf16[2048,4096]{1,0:T(8,128)(2,1)} %x_ref.5) | copy-start | bytes 50331652
  14.4 18.9 %copy-start.2 = (bf16[2048]{0:T(1024)(128)(2,1)S(1)}, bf16[2048]{0:T(1024)(128)(2,1)}, u32[]{:S(2)}) copy-start(bf16[2048]{0:T(1024)(128)(2,1)} %param.4) | copy-start | bytes 12292
  22.7 7.6 %collective-permute-start.3 = (bf16[512,256]{1,0:T(8,128)(2,1)S(1)}, bf16[512,256]{1,0:T(8,128)(2,1)S(1)}, u32[]{:S(2)}, u32[]{:S(2)}) collective-permute-start(bf16[512,256]{1,0:T(8,128)(2,1)S(1)} %get-tuple-element.10), channel_id=1, source_target_pairs={{0,2},{1,3},{2,4},{3,5},{4,6},{5,7},{6,0},{7,1},{8,10},{9,11},{10,... | collective-permute-start | bytes 786440 | tf_op jit(solution)/shard_map/ppermute | solution.py:290
  22.7 7.5 %collective-permute-start.4 = (bf16[512,256]{1,0:T(8,128)(2,1)S(1)}, bf16[512,256]{1,0:T(8,128)(2,1)S(1)}, u32[]{:S(2)}, u32[]{:S(2)}) collective-permute-start(bf16[512,256]{1,0:T(8,128)(2,1)S(1)} %get-tuple-element.11), channel_id=1, source_target_pairs={{0,6},{1,7},{2,0},{3,1},{4,2},{5,3},{6,4},{7,5},{8,14},{9,15},{10,... | collective-permute-start | bytes 786440 | tf_op jit(solution)/shard_map/ppermute | solution.py:290
  30.8 5.6 %collective-permute-start.5 = (bf16[1024,256]{1,0:T(8,128)(2,1)S(1)}, bf16[1024,256]{1,0:T(8,128)(2,1)S(1)}, u32[]{:S(2)}, u32[]{:S(2)}) collective-permute-start(bf16[1024,256]{1,0:T(8,128)(2,1)S(1)} %shard_map.52.block_ref), channel_id=1, source_target_pairs={{0,1},{1,0},{2,3},{3,2},{4,5},{5,4},{6,7},{7,6},{8,9},{9,8},{10,11... | collective-permute-start | bytes 1572872 | tf_op jit(solution)/shard_map/ppermute | solution.py:300

commit v6 on v5

--- a/solution.py
+++ b/solution.py
@@ -177,13 +177,14 @@
         acc = later
         if t + 1 < items // tile:
             later = whole(t + 1)
-        mrow = acc[P_SIZE : P_SIZE + 1, :] * inverse
-        moment = acc[0:P_SIZE, :] * inverse - pcol * mrow
+        colsum = acc[P_SIZE : P_SIZE + 1, :]
+        mrow = colsum * inverse
+        moment = acc[0:P_SIZE, :] - pcol * colsum
         top = jnp.max(jnp.max(jnp.abs(moment), axis=0, keepdims=True), axis=1, keepdims=True)
-        scale = (32768.0 / jnp.maximum(top, 1e-30)).astype(BF16).astype(F32)
+        scale = (8192.0 / jnp.maximum(top, 1e-30)).astype(BF16).astype(F32)
         v = moment * scale
-        v2 = v * v
-        coded = (v * jnp.abs(v) * v2 * (v2 * v2)).astype(BF16).T.reshape(pieces, BLK, P_SIZE)
+        v3 = v * v * v
+        coded = (v3 * v3 * v3).astype(BF16).T.reshape(pieces, BLK, P_SIZE)
         for k in range(pieces):
             place = slot(t * pieces + k)
             out_ref[place, 0:BLK, :] = coded[k, :, 0:LANES]
@@ -230,7 +231,8 @@
     panel = part(0) + part(2) + part(4)
     last = stats0[:, 7, :]
     count = last[:, 0:1] + last[:, 32:33] + last[:, 64:65]
-    share = count / jnp.sum(count, axis=0, keepdims=True)
+    everyone = jnp.sum(count, axis=0, keepdims=True)
+    share = count / everyone
     panel_dev = panel - jnp.sum(share * panel, axis=0, keepdims=True)
     for i in range(cycles):
         at = i % CORES * (cycles // CORES) + i // CORES
@@ -247,11 +249,11 @@
             precision=lax.Precision.HIGHEST,
             preferred_element_type=F32,
         )
-        back = share / stats[:, 7, 96:97]
+        back = 1.0 / (everyone * stats[:, 7, 96:97])
         within = jnp.zeros((2 * BLK, LANES), F32)
         for u in range(groups):
             y = in_ref[at, u, 0 : 2 * BLK, :].astype(F32)
-            shrink = jnp.exp2(-0.875 * jnp.log2(jnp.maximum(jnp.abs(y), 1e-37)))
+            shrink = jnp.exp2((-8.0 / 9.0) * jnp.log2(jnp.maximum(jnp.abs(y), 1e-37)))
             within = within + (y * back[u : u + 1, :]) * shrink
         first = within[0:BLK] + between[:, 0:LANES]
         second = within[BLK:] + between[:, LANES:]

time: 84.9 us -> 85 us (level)
  no operation moved by 1% of the time
where the time goes in v6:
time: 85 us; the launch traced here: 84.8 us
  blocking collectives  41.2 us (48%)
  waiting for transfers between devices  14.5 us (17%)
  Pallas kernels  10.8 us (13%)
  starting transfers between devices  9.65 us (11%)
  local copies, waits for them, and re-layouts  7.06 us (8%)
  between operations  1.38 us (2%)
    all_to_all x1, blocking collectives, per_device(): moved = lax.all_to_all(pieces, ORDER, 0, 0, tiled=True)  41.2 us
    ppermute x4, waiting for transfers between devices, step(): return lax.ppermute(block, ITEMS, pairs)  13 us
    unnamed x6, local copies, waits for them, and re-layouts  5.78 us
    ppermute x4, starting transfers between devices, step(): return lax.ppermute(block, ITEMS, pairs)  5.63 us
    pallas_call x1, Pallas kernels, moments(): pl.pallas_call(functools.partial(moment_kernel, tile), in_specs=[pl.Block...  4.7 us
    pallas_call x1, Pallas kernels, own_half(): pl.pallas_call(functools.partial(own_kernel, 512), in_specs=[pl.BlockSpec...  3.09 us
    ppermute x1, starting transfers between devices, spread_panel(): return (mine, lax.ppermute(mine, ITEMS, across))  2.53 us
    pallas_call x1, Pallas kernels, merge(): pl.pallas_call(functools.partial(merge_kernel, groups, cycles), out_shape...  2.41 us
  transfers between devices with their start and end apart: 6, of which 4 were waited for; matrix products, arithmetic and copies ran while one was open for 0% of the time, Pallas kernels for 4%

profile of v6, /device:TPU:1, one launch (start us, length us, event | category | flops | bytes accessed | tf_op | source)
XLA Modules:
  0.0 84.8 jit_solution(1079968735835932413)
XLA Ops:
  1.3 1.3 %fusion = (bf16[1024,256]{1,0:T(8,128)(2,1)S(1)}, bf16[1024,256]{1,0:T(8,128)(2,1)S(1)}) fusion(bf16[2048,4096]{1,0:T(8,128)(2,1)} %x_ref.5, s32[]{:T(128)S(6)} %select_n.57, s32[]{:T(128)S(6)} %select_n.56, s32[]{:T(128)S(6)} %select_n.54), kind=kLoop, calls=%fused_computation.2 | loop fusion | bytes 2097164 | tf_op jit(solution)/shard_map/dynamic_slice | solution.py:295
  2.6 1.5 %collective-permute-start = (bf16[1024,256]{1,0:T(8,128)(2,1)S(1)}, bf16[1024,256]{1,0:T(8,128)(2,1)S(1)}, u32[]{:S(2)}, u32[]{:S(2)}) collective-permute-start(bf16[1024,256]{1,0:T(8,128)(2,1)S(1)} %get-tuple-element.9), channel_id=1, source_target_pairs={{0,1},{1,0},{2,3},{3,2},{4,5},{5,4},{6,7},{7,6},{8,9},{9,8},{10,11... | collective-permute-start | bytes 1572872 | tf_op jit(solution)/shard_map/ppermute | solution.py:297
  4.1 1.5 %collective-permute-done = bf16[1024,256]{1,0:T(8,128)(2,1)S(1)} collective-permute-done((bf16[1024,256]{1,0:T(8,128)(2,1)S(1)}, bf16[1024,256]{1,0:T(8,128)(2,1)S(1)}, u32[]{:S(2)}, u32[]{:S(2)}) %collective-permute-start) | collective-permute-done | bytes 524320 | tf_op jit(solution)/shard_map/ppermute | solution.py:297
  5.7 0.1 broadcast_select_fusion.after_ref.mine_ref
  5.7 2.9 %collective-permute-start.2 = (bf16[1024,256]{1,0:T(8,128)(2,1)S(1)}, bf16[1024,256]{1,0:T(8,128)(2,1)S(1)}, u32[]{:S(2)}, u32[]{:S(2)}) collective-permute-start(bf16[1024,256]{1,0:T(8,128)(2,1)S(1)} %broadcast_select_fusion.after_ref.mine_ref), channel_id=1, source_target_pairs={{0,6},{1,7},{2,0},{3,1},{4,2},{5,3},{6,4},{7,5},{8,14},{9,15},{10,... | collective-permute-start | bytes 1572872 | tf_op jit(solution)/shard_map/ppermute | solution.py:292
  8.6 0.0 collective-permute-start.1
  8.6 0.1 pad_add_fusion.info_ref
  8.7 0.0 copy-start
  8.7 5.8 %copy-done = bf16[2048,4096]{1,0:T(8,128)(2,1)S(1)} copy-done((bf16[2048,4096]{1,0:T(8,128)(2,1)S(1)}, bf16[2048,4096]{1,0:T(8,128)(2,1)}, u32[]{:S(2)}) %copy-start) | copy-done | bytes 16777240
  14.4 0.0 copy-start.1
  14.4 0.0 copy-start.2
  14.5 5.1 %collective-permute-done.2.left_ref = bf16[1024,256]{1,0:T(8,128)(2,1)S(1)} collective-permute-done((bf16[1024,256]{1,0:T(8,128)(2,1)S(1)}, bf16[1024,256]{1,0:T(8,128)(2,1)S(1)}, u32[]{:S(2)}, u32[]{:S(2)}) %collective-permute-start.2) | collective-permute-done | bytes 524320 | tf_op jit(solution)/shard_map/ppermute | solution.py:292
  19.5 3.1 %collective-permute-done.1.right_ref = bf16[1024,256]{1,0:T(8,128)(2,1)S(1)} collective-permute-done((bf16[1024,256]{1,0:T(8,128)(2,1)S(1)}, bf16[1024,256]{1,0:T(8,128)(2,1)S(1)}, u32[]{:S(2)}, u32[]{:S(2)}) %collective-permute-start.1) | collective-permute-done | bytes 524320 | tf_op jit(solution)/shard_map/ppermute | solution.py:292
  22.7 0.1 collective-permute-start.3
  22.7 2.7 %collective-permute-start.4 = (bf16[512,256]{1,0:T(8,128)(2,1)S(1)}, bf16[512,256]{1,0:T(8,128)(2,1)S(1)}, u32[]{:S(2)}, u32[]{:S(2)}) collective-permute-start(bf16[512,256]{1,0:T(8,128)(2,1)S(1)} %get-tuple-element.11), channel_id=1, source_target_pairs={{0,6},{1,7},{2,0},{3,1},{4,2},{5,3},{6,4},{7,5},{8,14},{9,15},{10,... | collective-permute-start | bytes 786440 | tf_op jit(solution)/shard_map/ppermute | solution.py:292
  25.4 4.8 %collective-permute-done.3.far_a_ref = bf16[512,256]{1,0:T(8,128)(2,1)S(1)} collective-permute-done((bf16[512,256]{1,0:T(8,128)(2,1)S(1)}, bf16[512,256]{1,0:T(8,128)(2,1)S(1)}, u32[]{:S(2)}, u32[]{:S(2)}) %collective-permute-start.3) | collective-permute-done | bytes 262176 | tf_op jit(solution)/shard_map/ppermute | solution.py:292
  30.2 0.0 collective-permute-done.4.far_b_ref
  30.2 0.6 shard_map.52.block_ref
  30.8 2.5 %collective-permute-start.5 = (bf16[1024,256]{1,0:T(8,128)(2,1)S(1)}, bf16[1024,256]{1,0:T(8,128)(2,1)S(1)}, u32[]{:S(2)}, u32[]{:S(2)}) collective-permute-start(bf16[1024,256]{1,0:T(8,128)(2,1)S(1)} %shard_map.52.block_ref), channel_id=1, source_target_pairs={{0,1},{1,0},{2,3},{3,2},{4,5},{5,4},{6,7},{7,6},{8,9},{9,8},{10,11... | collective-permute-start | bytes 1572872 | tf_op jit(solution)/shard_map/ppermute | solution.py:302
  33.4 0.0 copy-done.1
  33.4 0.0 copy-done.2
  33.4 3.1 %shard_map.53 = (f32[272,4096]{1,0:T(8,128)S(1)}, f32[256,128]{1,0:T(8,128)S(1)}) custom-call(s32[2]{0:T(128)S(1)} %pad_add_fusion.info_ref, bf16[16,128]{1,0:T(8,128)(2,1)S(1)} %bitcast.10, bf16[1024,256]{1,0:T(8,128)(2,1)S(1)} %shard_map.52.block_ref, bf16[2048,4096]{1,0:T(8,128)(2,1)S(1)} %copy-done.1), custom_call_target="tpu_custom_call" | custom-call | flops 2147483648 | bytes 4194304 | tf_op jit(solution)/shard_map/pallas_call | solution.py:128
  36.5 0.0 collective-permute-done.5.block_ref
  36.5 4.7 %shard_map.54 = bf16[128,72,128]{2,1,0:T(8,128)(2,1)S(1)} custom-call(s32[2]{0:T(128)S(1)} %pad_add_fusion.info_ref, bf16[16,128]{1,0:T(8,128)(2,1)S(1)} %bitcast.11, bf16[1024,256]{1,0:T(8,128)(2,1)S(1)} %collective-permute-done.5.block_ref, bf16[2048,4096]{1,0:T(8,128)(2,1)S(1)} %copy-done.1, f32[272,4096]{1,0:T(8,128)S(1)} %get-tuple-element.12.acc_ref, ...), custom_call_target="tpu_custom_call" | custom-call | flops 2147483648 | bytes 4194304 | tf_op jit(solution)/shard_map/pallas_call | solution.py:214
  41.2 41.2 %all_to_all.5 = bf16[128,72,128]{2,1,0:T(8,128)(2,1)S(1)} all-to-all(bf16[128,72,128]{2,1,0:T(8,128)(2,1)S(1)} %shard_map.54), channel_id=1, replica_groups=mesh['z'=4,'x'=4,'y'=4,'c'=2] {'c','y','x','z'}, dimensions={0} | all-to-all | bytes 4718592 | tf_op jit(solution)/shard_map/all_to_all | solution.py:316
  82.4 2.4 %shard_map.55 = (f32[8,32,256]{2,1,0:T(8,128)}, f32[8,32]{1,0:T(8,128)}) custom-call(bf16[8,16,72,128]{3,2,1,0:T(8,128)(2,1)S(1)} %bitcast.9), custom_call_target="tpu_custom_call" | custom-call | flops 20971520 | bytes 3145728 | tf_op jit(solution)/shard_map/pallas_call | solution.py:265
  (2 shorter events, 0.0 us)
Async XLA Ops:
  2.6 3.0 %collective-permute-start = (bf16[1024,256]{1,0:T(8,128)(2,1)S(1)}, bf16[1024,256]{1,0:T(8,128)(2,1)S(1)}, u32[]{:S(2)}, u32[]{:S(2)}) collective-permute-start(bf16[1024,256]{1,0:T(8,128)(2,1)S(1)} %get-tuple-element.9), channel_id=1, source_target_pairs={{0,1},{1,0},{2,3},{3,2},{4,5},{5,4},{6,7},{7,6},{8,9},{9,8},{10,11... | collective-permute-start | bytes 1572872 | tf_op jit(solution)/shard_map/ppermute | solution.py:297
  5.7 13.8 %collective-permute-start.2 = (bf16[1024,256]{1,0:T(8,128)(2,1)S(1)}, bf16[1024,256]{1,0:T(8,128)(2,1)S(1)}, u32[]{:S(2)}, u32[]{:S(2)}) collective-permute-start(bf16[1024,256]{1,0:T(8,128)(2,1)S(1)} %broadcast_select_fusion.after_ref.mine_ref), channel_id=1, source_target_pairs={{0,6},{1,7},{2,0},{3,1},{4,2},{5,3},{6,4},{7,5},{8,14},{9,15},{10,... | collective-permute-start | bytes 1572872 | tf_op jit(solution)/shard_map/ppermute | solution.py:292
  8.6 14.0 %collective-permute-start.1 = (bf16[1024,256]{1,0:T(8,128)(2,1)S(1)}, bf16[1024,256]{1,0:T(8,128)(2,1)S(1)}, u32[]{:S(2)}, u32[]{:S(2)}) collective-permute-start(bf16[1024,256]{1,0:T(8,128)(2,1)S(1)} %broadcast_select_fusion.after_ref.mine_ref), channel_id=1, source_target_pairs={{0,2},{1,3},{2,4},{3,5},{4,6},{5,7},{6,0},{7,1},{8,10},{9,11},{10,... | collective-permute-start | bytes 1572872 | tf_op jit(solution)/shard_map/ppermute | solution.py:292
  8.7 5.8 %copy-start = (bf16[2048,4096]{1,0:T(8,128)(2,1)S(1)}, bf16[2048,4096]{1,0:T(8,128)(2,1)}, u32[]{:S(2)}) copy-start(bf16[2048,4096]{1,0:T(8,128)(2,1)} %x_ref.5) | copy-start | bytes 50331652
  14.4 18.9 %copy-start.1 = (bf16[2048,4096]{1,0:T(8,128)(2,1)S(1)}, bf16[2048,4096]{1,0:T(8,128)(2,1)}, u32[]{:S(2)}) copy-start(bf16[2048,4096]{1,0:T(8,128)(2,1)} %x_ref.5) | copy-start | bytes 50331652
  14.4 18.9 %copy-start.2 = (bf16[2048]{0:T(1024)(128)(2,1)S(1)}, bf16[2048]{0:T(1024)(128)(2,1)}, u32[]{:S(2)}) copy-start(bf16[2048]{0:T(1024)(128)(2,1)} %param.4) | copy-start | bytes 12292
  22.7 7.6 %collective-permute-start.3 = (bf16[512,256]{1,0:T(8,128)(2,1)S(1)}, bf16[512,256]{1,0:T(8,128)(2,1)S(1)}, u32[]{:S(2)}, u32[]{:S(2)}) collective-permute-start(bf16[512,256]{1,0:T(8,128)(2,1)S(1)} %get-tuple-element.10), channel_id=1, source_target_pairs={{0,2},{1,3},{2,4},{3,5},{4,6},{5,7},{6,0},{7,1},{8,10},{9,11},{10,... | collective-permute-start | bytes 786440 | tf_op jit(solution)/shard_map/ppermute | solution.py:292
  22.7 7.5 %collective-permute-start.4 = (bf16[512,256]{1,0:T(8,128)(2,1)S(1)}, bf16[512,256]{1,0:T(8,128)(2,1)S(1)}, u32[]{:S(2)}, u32[]{:S(2)}) collective-permute-start(bf16[512,256]{1,0:T(8,128)(2,1)S(1)} %get-tuple-element.11), channel_id=1, source_target_pairs={{0,6},{1,7},{2,0},{3,1},{4,2},{5,3},{6,4},{7,5},{8,14},{9,15},{10,... | collective-permute-start | bytes 786440 | tf_op jit(solution)/shard_map/ppermute | solution.py:292
  30.8 5.6 %collective-permute-start.5 = (bf16[1024,256]{1,0:T(8,128)(2,1)S(1)}, bf16[1024,256]{1,0:T(8,128)(2,1)S(1)}, u32[]{:S(2)}, u32[]{:S(2)}) collective-permute-start(bf16[1024,256]{1,0:T(8,128)(2,1)S(1)} %shard_map.52.block_ref), channel_id=1, source_target_pairs={{0,1},{1,0},{2,3},{3,2},{4,5},{5,4},{6,7},{7,6},{8,9},{9,8},{10,11... | collective-permute-start | bytes 1572872 | tf_op jit(solution)/shard_map/ppermute | solution.py:302

commit v7 on v5

--- a/solution.py
+++ b/solution.py
@@ -291,7 +291,7 @@
 
     own = lax.dynamic_slice(x, (core * half, start), (half, P_SIZE))
     other = lax.dynamic_slice(x, ((1 - core) * half, start), (half, P_SIZE))
-    own, other = lax.optimization_barrier((own, other))
+    own = lax.optimization_barrier(own)
     mine = jnp.where(same, own, lax.ppermute(other, ITEMS, across))
     right, left = step(mine, 1), step(mine, -1)
     first, second = turn(right, left, touch(x, mine, info))

time: 84.9 us -> 84.9 us (level)
  no operation moved by 1% of the time
where the time goes in v7:
time: 84.9 us; the launch traced here: 84.7 us
  blocking collectives  41.2 us (49%)
  waiting for transfers between devices  14.5 us (17%)
  Pallas kernels  10.8 us (13%)
  starting transfers between devices  9.65 us (11%)
  local copies, waits for them, and re-layouts  7.06 us (8%)
  between operations  1.38 us (2%)
    all_to_all x1, blocking collectives, per_device(): moved = lax.all_to_all(pieces, ORDER, 0, 0, tiled=True)  41.2 us
    ppermute x4, waiting for transfers between devices, step(): return lax.ppermute(block, ITEMS, pairs)  13 us
    unnamed x6, local copies, waits for them, and re-layouts  5.78 us
    ppermute x4, starting transfers between devices, step(): return lax.ppermute(block, ITEMS, pairs)  5.63 us
    pallas_call x1, Pallas kernels, moments(): pl.pallas_call(functools.partial(moment_kernel, tile), in_specs=[pl.Block...  4.62 us
    pallas_call x1, Pallas kernels, own_half(): pl.pallas_call(functools.partial(own_kernel, 512), in_specs=[pl.BlockSpec...  3.09 us
    ppermute x1, starting transfers between devices, spread_panel(): return (mine, lax.ppermute(mine, ITEMS, across))  2.53 us
    pallas_call x1, Pallas kernels, merge(): pl.pallas_call(functools.partial(merge_kernel, groups, cycles), out_shape...  2.42 us
  transfers between devices with their start and end apart: 6, of which 4 were waited for; matrix products, arithmetic and copies ran while one was open for 0% of the time, Pallas kernels for 4%

profile of v7, /device:TPU:1, one launch (start us, length us, event | category | flops | bytes accessed | tf_op | source)
XLA Modules:
  0.0 84.7 jit_solution(10062417195277732321)
XLA Ops:
  1.3 1.3 %fusion = (bf16[1024,256]{1,0:T(8,128)(2,1)S(1)}, bf16[1024,256]{1,0:T(8,128)(2,1)S(1)}) fusion(bf16[2048,4096]{1,0:T(8,128)(2,1)} %x_ref.5, s32[]{:T(128)S(6)} %select_n.57, s32[]{:T(128)S(6)} %select_n.56, s32[]{:T(128)S(6)} %select_n.54), kind=kLoop, calls=%fused_computation.2 | loop fusion | bytes 2097164 | tf_op jit(solution)/shard_map/dynamic_slice | solution.py:293
  2.6 1.5 %collective-permute-start = (bf16[1024,256]{1,0:T(8,128)(2,1)S(1)}, bf16[1024,256]{1,0:T(8,128)(2,1)S(1)}, u32[]{:S(2)}, u32[]{:S(2)}) collective-permute-start(bf16[1024,256]{1,0:T(8,128)(2,1)S(1)} %get-tuple-element.10), channel_id=1, source_target_pairs={{0,1},{1,0},{2,3},{3,2},{4,5},{5,4},{6,7},{7,6},{8,9},{9,8},{10,11... | collective-permute-start | bytes 1572872 | tf_op jit(solution)/shard_map/ppermute | solution.py:295
  4.1 1.5 %collective-permute-done = bf16[1024,256]{1,0:T(8,128)(2,1)S(1)} collective-permute-done((bf16[1024,256]{1,0:T(8,128)(2,1)S(1)}, bf16[1024,256]{1,0:T(8,128)(2,1)S(1)}, u32[]{:S(2)}, u32[]{:S(2)}) %collective-permute-start) | collective-permute-done | bytes 524320 | tf_op jit(solution)/shard_map/ppermute | solution.py:295
  5.7 0.1 broadcast_select_fusion.after_ref.mine_ref
  5.7 2.9 %collective-permute-start.2 = (bf16[1024,256]{1,0:T(8,128)(2,1)S(1)}, bf16[1024,256]{1,0:T(8,128)(2,1)S(1)}, u32[]{:S(2)}, u32[]{:S(2)}) collective-permute-start(bf16[1024,256]{1,0:T(8,128)(2,1)S(1)} %broadcast_select_fusion.after_ref.mine_ref), channel_id=1, source_target_pairs={{0,6},{1,7},{2,0},{3,1},{4,2},{5,3},{6,4},{7,5},{8,14},{9,15},{10,... | collective-permute-start | bytes 1572872 | tf_op jit(solution)/shard_map/ppermute | solution.py:290
  8.6 0.0 collective-permute-start.1
  8.6 0.1 pad_add_fusion.info_ref
  8.7 0.0 copy-start
  8.7 5.8 %copy-done = bf16[2048,4096]{1,0:T(8,128)(2,1)S(1)} copy-done((bf16[2048,4096]{1,0:T(8,128)(2,1)S(1)}, bf16[2048,4096]{1,0:T(8,128)(2,1)}, u32[]{:S(2)}) %copy-start) | copy-done | bytes 16777240
  14.4 0.0 copy-start.1
  14.4 0.0 copy-start.2
  14.5 5.1 %collective-permute-done.2.left_ref = bf16[1024,256]{1,0:T(8,128)(2,1)S(1)} collective-permute-done((bf16[1024,256]{1,0:T(8,128)(2,1)S(1)}, bf16[1024,256]{1,0:T(8,128)(2,1)S(1)}, u32[]{:S(2)}, u32[]{:S(2)}) %collective-permute-start.2) | collective-permute-done | bytes 524320 | tf_op jit(solution)/shard_map/ppermute | solution.py:290
  19.5 3.1 %collective-permute-done.1.right_ref = bf16[1024,256]{1,0:T(8,128)(2,1)S(1)} collective-permute-done((bf16[1024,256]{1,0:T(8,128)(2,1)S(1)}, bf16[1024,256]{1,0:T(8,128)(2,1)S(1)}, u32[]{:S(2)}, u32[]{:S(2)}) %collective-permute-start.1) | collective-permute-done | bytes 524320 | tf_op jit(solution)/shard_map/ppermute | solution.py:290
  22.7 0.1 collective-permute-start.3
  22.7 2.7 %collective-permute-start.4 = (bf16[512,256]{1,0:T(8,128)(2,1)S(1)}, bf16[512,256]{1,0:T(8,128)(2,1)S(1)}, u32[]{:S(2)}, u32[]{:S(2)}) collective-permute-start(bf16[512,256]{1,0:T(8,128)(2,1)S(1)} %get-tuple-element.7), channel_id=1, source_target_pairs={{0,6},{1,7},{2,0},{3,1},{4,2},{5,3},{6,4},{7,5},{8,14},{9,15},{10,... | collective-permute-start | bytes 786440 | tf_op jit(solution)/shard_map/ppermute | solution.py:290
  25.4 4.8 %collective-permute-done.3.far_a_ref = bf16[512,256]{1,0:T(8,128)(2,1)S(1)} collective-permute-done((bf16[512,256]{1,0:T(8,128)(2,1)S(1)}, bf16[512,256]{1,0:T(8,128)(2,1)S(1)}, u32[]{:S(2)}, u32[]{:S(2)}) %collective-permute-start.3) | collective-permute-done | bytes 262176 | tf_op jit(solution)/shard_map/ppermute | solution.py:290
  30.2 0.0 collective-permute-done.4.far_b_ref
  30.2 0.6 shard_map.52.block_ref
  30.8 2.5 %collective-permute-start.5 = (bf16[1024,256]{1,0:T(8,128)(2,1)S(1)}, bf16[1024,256]{1,0:T(8,128)(2,1)S(1)}, u32[]{:S(2)}, u32[]{:S(2)}) collective-permute-start(bf16[1024,256]{1,0:T(8,128)(2,1)S(1)} %shard_map.52.block_ref), channel_id=1, source_target_pairs={{0,1},{1,0},{2,3},{3,2},{4,5},{5,4},{6,7},{7,6},{8,9},{9,8},{10,11... | collective-permute-start | bytes 1572872 | tf_op jit(solution)/shard_map/ppermute | solution.py:300
  33.4 0.0 copy-done.1
  33.4 0.0 copy-done.2
  33.4 3.1 %shard_map.53 = (f32[272,4096]{1,0:T(8,128)S(1)}, f32[256,128]{1,0:T(8,128)S(1)}) custom-call(s32[2]{0:T(128)S(1)} %pad_add_fusion.info_ref, bf16[16,128]{1,0:T(8,128)(2,1)S(1)} %bitcast.10, bf16[1024,256]{1,0:T(8,128)(2,1)S(1)} %shard_map.52.block_ref, bf16[2048,4096]{1,0:T(8,128)(2,1)S(1)} %copy-done.1), custom_call_target="tpu_custom_call" | custom-call | flops 2147483648 | bytes 4194304 | tf_op jit(solution)/shard_map/pallas_call | solution.py:128
  36.5 0.0 collective-permute-done.5.block_ref
  36.5 4.6 %shard_map.54 = bf16[128,72,128]{2,1,0:T(8,128)(2,1)S(1)} custom-call(s32[2]{0:T(128)S(1)} %pad_add_fusion.info_ref, bf16[16,128]{1,0:T(8,128)(2,1)S(1)} %bitcast.11, bf16[1024,256]{1,0:T(8,128)(2,1)S(1)} %collective-permute-done.5.block_ref, bf16[2048,4096]{1,0:T(8,128)(2,1)S(1)} %copy-done.1, f32[272,4096]{1,0:T(8,128)S(1)} %get-tuple-element.8.acc_ref, ...), custom_call_target="tpu_custom_call" | custom-call | flops 2147483648 | bytes 4194304 | tf_op jit(solution)/shard_map/pallas_call | solution.py:213
  41.1 41.2 %all_to_all.5 = bf16[128,72,128]{2,1,0:T(8,128)(2,1)S(1)} all-to-all(bf16[128,72,128]{2,1,0:T(8,128)(2,1)S(1)} %shard_map.54), channel_id=1, replica_groups=mesh['z'=4,'x'=4,'y'=4,'c'=2] {'c','y','x','z'}, dimensions={0} | all-to-all | bytes 4718592 | tf_op jit(solution)/shard_map/all_to_all | solution.py:314
  82.3 2.4 %shard_map.55 = (f32[8,32,256]{2,1,0:T(8,128)}, f32[8,32]{1,0:T(8,128)}) custom-call(bf16[8,16,72,128]{3,2,1,0:T(8,128)(2,1)S(1)} %bitcast.9), custom_call_target="tpu_custom_call" | custom-call | flops 20971520 | bytes 3145728 | tf_op jit(solution)/shard_map/pallas_call | solution.py:263
  (2 shorter events, 0.0 us)
Async XLA Ops:
  2.6 3.0 %collective-permute-start = (bf16[1024,256]{1,0:T(8,128)(2,1)S(1)}, bf16[1024,256]{1,0:T(8,128)(2,1)S(1)}, u32[]{:S(2)}, u32[]{:S(2)}) collective-permute-start(bf16[1024,256]{1,0:T(8,128)(2,1)S(1)} %get-tuple-element.10), channel_id=1, source_target_pairs={{0,1},{1,0},{2,3},{3,2},{4,5},{5,4},{6,7},{7,6},{8,9},{9,8},{10,11... | collective-permute-start | bytes 1572872 | tf_op jit(solution)/shard_map/ppermute | solution.py:295
  5.7 13.8 %collective-permute-start.2 = (bf16[1024,256]{1,0:T(8,128)(2,1)S(1)}, bf16[1024,256]{1,0:T(8,128)(2,1)S(1)}, u32[]{:S(2)}, u32[]{:S(2)}) collective-permute-start(bf16[1024,256]{1,0:T(8,128)(2,1)S(1)} %broadcast_select_fusion.after_ref.mine_ref), channel_id=1, source_target_pairs={{0,6},{1,7},{2,0},{3,1},{4,2},{5,3},{6,4},{7,5},{8,14},{9,15},{10,... | collective-permute-start | bytes 1572872 | tf_op jit(solution)/shard_map/ppermute | solution.py:290
  8.6 14.0 %collective-permute-start.1 = (bf16[1024,256]{1,0:T(8,128)(2,1)S(1)}, bf16[1024,256]{1,0:T(8,128)(2,1)S(1)}, u32[]{:S(2)}, u32[]{:S(2)}) collective-permute-start(bf16[1024,256]{1,0:T(8,128)(2,1)S(1)} %broadcast_select_fusion.after_ref.mine_ref), channel_id=1, source_target_pairs={{0,2},{1,3},{2,4},{3,5},{4,6},{5,7},{6,0},{7,1},{8,10},{9,11},{10,... | collective-permute-start | bytes 1572872 | tf_op jit(solution)/shard_map/ppermute | solution.py:290
  8.7 5.8 %copy-start = (bf16[2048,4096]{1,0:T(8,128)(2,1)S(1)}, bf16[2048,4096]{1,0:T(8,128)(2,1)}, u32[]{:S(2)}) copy-start(bf16[2048,4096]{1,0:T(8,128)(2,1)} %x_ref.5) | copy-start | bytes 50331652
  14.4 18.9 %copy-start.1 = (bf16[2048,4096]{1,0:T(8,128)(2,1)S(1)}, bf16[2048,4096]{1,0:T(8,128)(2,1)}, u32[]{:S(2)}) copy-start(bf16[2048,4096]{1,0:T(8,128)(2,1)} %x_ref.5) | copy-start | bytes 50331652
  14.4 18.9 %copy-start.2 = (bf16[2048]{0:T(1024)(128)(2,1)S(1)}, bf16[2048]{0:T(1024)(128)(2,1)}, u32[]{:S(2)}) copy-start(bf16[2048]{0:T(1024)(128)(2,1)} %param.4) | copy-start | bytes 12292
  22.7 7.6 %collective-permute-start.3 = (bf16[512,256]{1,0:T(8,128)(2,1)S(1)}, bf16[512,256]{1,0:T(8,128)(2,1)S(1)}, u32[]{:S(2)}, u32[]{:S(2)}) collective-permute-start(bf16[512,256]{1,0:T(8,128)(2,1)S(1)} %get-tuple-element.6), channel_id=1, source_target_pairs={{0,2},{1,3},{2,4},{3,5},{4,6},{5,7},{6,0},{7,1},{8,10},{9,11},{10,... | collective-permute-start | bytes 786440 | tf_op jit(solution)/shard_map/ppermute | solution.py:290
  22.7 7.5 %collective-permute-start.4 = (bf16[512,256]{1,0:T(8,128)(2,1)S(1)}, bf16[512,256]{1,0:T(8,128)(2,1)S(1)}, u32[]{:S(2)}, u32[]{:S(2)}) collective-permute-start(bf16[512,256]{1,0:T(8,128)(2,1)S(1)} %get-tuple-element.7), channel_id=1, source_target_pairs={{0,6},{1,7},{2,0},{3,1},{4,2},{5,3},{6,4},{7,5},{8,14},{9,15},{10,... | collective-permute-start | bytes 786440 | tf_op jit(solution)/shard_map/ppermute | solution.py:290
  30.8 5.6 %collective-permute-start.5 = (bf16[1024,256]{1,0:T(8,128)(2,1)S(1)}, bf16[1024,256]{1,0:T(8,128)(2,1)S(1)}, u32[]{:S(2)}, u32[]{:S(2)}) collective-permute-start(bf16[1024,256]{1,0:T(8,128)(2,1)S(1)} %shard_map.52.block_ref), channel_id=1, source_target_pairs={{0,1},{1,0},{2,3},{3,2},{4,5},{5,4},{6,7},{7,6},{8,9},{9,8},{10,11... | collective-permute-start | bytes 1572872 | tf_op jit(solution)/shard_map/ppermute | solution.py:300
